TPU v7x, 32 devices: a whole 2x2x4 slice. The times are simulated.
32 devices in a mesh: groups: 2 (over y), ffn: 4 (over z), width: 2 (over x), sub: 2 (over core).
Axes of the slice: x: 2, y: 2, z: 4, core: 2. Of those that a mesh axis runs over, the one named last changes fastest.
Arguments:
- tokens: bfloat16 [32, 16384], P(('groups', 'ffn'), ('width', 'sub')), parts along dimension 0, may hold values from -2000 to 2000
- norm_gain: bfloat16 [16384], P(('width', 'sub')), may hold values from 0.5 to 1.5
- w_qkv: bfloat16 [16384, 9216], P(('width', 'sub'), 'ffn'), may hold values from -0.046875 to 0.046875
- w_out: bfloat16 [8192, 16384], P('ffn', ('width', 'sub')), may hold values from -0.0625 to 0.0625
- kv_cache: bfloat16 [2, 32, 4096, 512], P(None, ('groups', 'width', 'sub'), 'ffn'), parts along dimension 1, may hold values from -64 to 64
- lengths: int32 [32], P(('groups', 'width', 'sub')), parts along dimension 0, may hold values from 1 to 4096, as said below
Outputs:
- attn_out: bfloat16 [32, 16384], P(('groups', 'ffn'), ('width', 'sub')), parts along dimension 0
There are 2 independent parts, one for each index of `groups`. A program takes and returns all parts, laid end to end along the dimension named above; an argument that names none is the same for every part. Nothing has to cross between parts.
Inputs may be any that keep to these rules, and one draw needn't show every extreme that they name: lengths[r] positions of row r's cache hold data, from position 0 on; some row has exactly 4096.
All inputs are finite; a program needn't handle non-finite values.
Results may differ from a plain program's by a relative error of at most 0.012.
Values may be sent and summed in bfloat16 or wider, within the bound.
No kernel may reach another device: no remote copies, remote signals or barrier semaphores. Data moves between devices by JAX's collectives and lax.ppermute only.
A program may use at most 128 MiB of HBM per device.

v0:
```python
import math

import jax
import jax.numpy as jnp
from jax import lax
from jax.sharding import PartitionSpec as P

D = 16384
HQ = 64
KVH = 4
DH = 128


def rotate(values, positions):
    half_dim = DH // 2
    frequency = 500000.0 ** (-(jnp.arange(half_dim, dtype=jnp.float32) * 2.0 / DH))
    angles = positions * frequency
    cosine = jnp.cos(angles)
    sine_part = jnp.sin(angles)
    first_half = values[..., :half_dim]
    second_half = values[..., half_dim:]
    return jnp.concatenate(
        [
            first_half * cosine - second_half * sine_part,
            second_half * cosine + first_half * sine_part,
        ],
        axis=-1,
    )


def local(tokens, norm_gain, w_qkv, w_out, kv_cache, lengths):
    widened = tokens.astype(jnp.float32)
    squares = lax.psum(jnp.sum(widened * widened, axis=1), ("width", "sub"))
    inverse_rms = 1.0 / jnp.sqrt(squares / D + 1e-05)
    normed = (widened * inverse_rms[:, None] * norm_gain.astype(jnp.float32)[None, :]).astype(
        jnp.bfloat16
    )
    gathered = lax.all_gather(normed, "ffn", axis=0, tiled=True)
    att_rows = kv_cache.shape[1]
    block_len = kv_cache.shape[2]
    qkv_part = lax.psum_scatter(
        jnp.dot(gathered, w_qkv, preferred_element_type=jnp.float32),
        ("width", "sub"),
        scatter_dimension=0,
        tiled=True,
    ).astype(jnp.bfloat16)
    qkv = lax.all_gather(qkv_part, "ffn", axis=1, tiled=True)
    group_size = HQ // KVH
    queries = qkv[:, : HQ * DH].astype(jnp.float32).reshape(att_rows, HQ, DH)
    new_keys = qkv[:, HQ * DH : (HQ + KVH) * DH].astype(jnp.float32).reshape(att_rows, KVH, DH)
    new_values = qkv[:, (HQ + KVH) * DH :].reshape(att_rows, KVH, DH)
    positions = lengths.astype(jnp.float32)[:, None, None]
    queries = rotate(queries, positions).astype(jnp.bfloat16)
    new_keys = rotate(new_keys, positions).astype(jnp.bfloat16)
    score_scale = 1.0 / math.sqrt(DH)
    grouped = queries.reshape(att_rows, KVH, group_size, DH)
    cached_keys = kv_cache[0].reshape(att_rows, block_len, KVH, DH)
    cached_values = kv_cache[1].reshape(att_rows, block_len, KVH, DH)
    scores = (
        jnp.einsum("rgqd,rpgd->rgqp", grouped, cached_keys, preferred_element_type=jnp.float32)
        * score_scale
    )
    cache_positions = lax.axis_index("ffn") * block_len + jnp.arange(block_len, dtype=jnp.int32)
    valid_mask = (cache_positions[None, :] < lengths[:, None])[:, None, None, :]
    block_top = jnp.max(jnp.where(valid_mask, scores, -1e30), axis=-1)
    overall_top = lax.pmax(block_top, "ffn")
    own_scores = (
        jnp.einsum("rgqd,rgd->rgq", grouped, new_keys, preferred_element_type=jnp.float32)
        * score_scale
    )
    top = jnp.maximum(overall_top, own_scores)
    probs = jnp.where(valid_mask, jnp.exp(scores - top[..., None]), 0.0)
    totals = jnp.sum(probs, axis=-1).reshape(att_rows, HQ)
    weighted = jnp.einsum(
        "rgqp,rpgd->rgqd",
        probs.astype(jnp.bfloat16),
        cached_values,
        preferred_element_type=jnp.float32,
    )
    weighted = weighted.reshape(att_rows, HQ, DH)
    head_count = HQ // lax.axis_size("ffn")
    head_start = lax.axis_index("ffn") * head_count
    weighted_mine, totals_mine = (
        lax.psum_scatter(weighted, "ffn", scatter_dimension=1, tiled=True),
        lax.psum_scatter(totals, "ffn", scatter_dimension=1, tiled=True),
    )
    own_probs = jnp.exp(own_scores - top).reshape(att_rows, HQ)
    own_mine = lax.dynamic_slice_in_dim(own_probs, head_start, head_count, 1)
    value_heads = jnp.repeat(new_values, group_size, axis=1)
    value_mine = lax.dynamic_slice_in_dim(value_heads, head_start, head_count, 1)
    weighted_mine = weighted_mine + own_mine.astype(jnp.bfloat16).astype(jnp.float32)[
        ..., None
    ] * value_mine.astype(jnp.float32)
    totals_mine = totals_mine + own_mine
    attention = (
        (weighted_mine / totals_mine[..., None])
        .astype(jnp.bfloat16)
        .reshape(att_rows, head_count * DH)
    )
    rows_all = lax.all_gather(attention, ("width", "sub"), axis=0, tiled=True)
    out_rows = tokens.shape[0]
    partial_all = jnp.dot(rows_all, w_out, preferred_element_type=jnp.float32)
    summed_all = lax.psum(partial_all, "ffn")
    row_start = lax.axis_index("ffn") * out_rows
    return lax.dynamic_slice_in_dim(summed_all, row_start, out_rows, 0).astype(jnp.bfloat16)


def solution(mesh):
    placed = (
        P(("groups", "ffn"), ("width", "sub")),
        P(("width", "sub")),
        P(("width", "sub"), "ffn"),
        P("ffn", ("width", "sub")),
        P(None, ("groups", "width", "sub"), "ffn", None),
        P(("groups", "width", "sub")),
    )
    return jax.shard_map(
        local,
        mesh=mesh,
        in_specs=placed,
        out_specs=P(("groups", "ffn"), ("width", "sub")),
        check_vma=False,
    )
```

profile of v0, /device:TPU:0, one launch (start us, length us, event | category | flops | bytes accessed | tf_op | source)
XLA Modules:
  0.0 174.8 jit_solution(17254308130437896264)
XLA Ops:
  6.5 0.0 reduce-scatter.7.cloned.1.call-start
  6.5 0.9 fusion.7
  7.5 0.7 convert_element_type.39
  8.2 8.3 %psum.14 = f32[4]{0:T(128)S(1)} all-reduce(f32[4]{0:T(128)S(1)} %fusion.7), channel_id=1, replica_groups=mesh['groups'=2,'ffn'=4,'width'=2,'sub'=2] {'width','sub'}, use_global_device_ids=true, to_apply=%region_1.0 | all-reduce | flops 4 | bytes 32 | tf_op jit(solution)/shard_map/psum | solution.py:33
  16.5 0.8 fusion.10
  17.3 13.6 %all-gather = bf16[4,4,4096]{2,1,0:T(4,128)(2,1)S(1)} all-gather(bf16[1,4,4096]{2,1,0:T(4,128)(2,1)S(1)} %fusion.10), channel_id=1, replica_groups=mesh['groups'=2,'ffn'=4,'width'=2,'sub'=2] {'ffn'}, dimensions={0}, use_global_device_ids=true | all-gather | bytes 163840 | tf_op jit(solution)/shard_map/all_gather | solution.py:38
  31.0 0.0 copy-start.1
  31.0 8.9 %fusion.19 = f32[16,2304]{1,0:T(8,128)S(1)} fusion(bf16[16,4096]{1,0:T(8,128)(2,1)S(1)} %reshape.142, bf16[4096,2304]{1,0:T(8,128)(2,1)} %param.8), kind=kOutput, calls=%fused_computation.45 | convolution fusion | flops 301989888 | bytes 19152896 | tf_op jit(solution)/shard_map/dot_general | solution.py:42
  39.9 12.0 %all-reduce.3 = bf16[16,2304]{1,0:T(8,128)(2,1)S(1)} all-reduce(f32[16,2304]{1,0:T(8,128)S(1)} %fusion.19), channel_id=2, replica_groups=mesh['groups'=2,'ffn'=4,'width'=2,'sub'=2] {'width','sub'}, use_global_device_ids=true, to_apply=%region_2.0.clone | all-reduce | flops 36864 | bytes 221184
  51.9 0.0 copy-done.1
  51.9 0.6 dynamic-slice
  53.2 13.2 %all_gather.10 = bf16[4,9216]{1,0:T(4,128)(2,1)S(1)} all-gather(bf16[4,2304]{1,0:T(4,128)(2,1)S(1)} %dynamic-slice_convert_fusion.1), channel_id=1, replica_groups=mesh['groups'=2,'ffn'=4,'width'=2,'sub'=2] {'ffn'}, dimensions={1}, use_global_device_ids=true | all-gather | bytes 92160 | tf_op jit(solution)/shard_map/all_gather | solution.py:47
  66.4 0.0 copy-start
  66.4 5.7 %fusion.17 = (bf16[1,4,1024,512]{3,2,1,0:T(8,128)(2,1)}, bf16[1,4,1024,512]{3,2,1,0:T(8,128)(2,1)}) fusion(bf16[2,4,1024,512]{3,2,1,0:T(8,128)(2,1)} %param.10), kind=kLoop, calls=%fused_computation.43 | loop fusion | bytes 16777216 | tf_op jit(solution)/shard_map/slice | solution.py:57
  72.1 0.0 copy-done
  72.1 0.1 broadcast_compare_fusion
  72.2 6.4 %copy.22 = bf16[1,4,1024,512]{2,3,1,0:T(8,128)(2,1)} copy(bf16[1,4,1024,512]{3,2,1,0:T(8,128)(2,1)} %get-tuple-element.5) | data formatting | bytes 8388608
  78.6 0.1 multiply_cosine_fusion
  78.7 0.1 subtract_convert_fusion
  78.8 0.1 subtract_convert_fusion.1
  78.9 0.1 maximum_bitcast_fusion
  79.0 0.2 fusion.11
  79.2 3.0 %select_reduce_fusion = (f32[4,4,16]{2,1,0:T(4,128)S(1)}, f32[4,4,16,1024]{3,2,1,0:T(8,128)S(1)}) fusion(pred[4,1024]{1,0:T(4,128)(4,1)S(1)} %broadcast_compare_fusion, bf16[4,1024,4,128]{1,3,2,0:T(8,128)(2,1)} %bitcast.28, bf16[4,4,16,64]{3,2,1,0:T(8,128)(2,1)S(1)} %bitcast.35, bf16[4,4,16,64]{3,2,1,0:T(8,128)(2,1)S(1)} %bitcast.33), kind=kOutput, calls=%fused_computation.2 | convolution fusion | flops 68026112 | bytes 5313536 | tf_op jit(solution)/shard_map/rgqd,rpgd->rgqp/dot_general | solution.py:60
  82.2 12.0 %pmax.7 = f32[4,4,16]{2,1,0:T(4,128)S(1)} all-reduce(f32[4,4,16]{2,1,0:T(4,128)S(1)} %get-tuple-element.17), channel_id=1, replica_groups=mesh['groups'=2,'ffn'=4,'width'=2,'sub'=2] {'ffn'}, use_global_device_ids=true, to_apply=%region_4.5 | all-reduce | flops 256 | bytes 2048 | tf_op jit(solution)/shard_map/pmax | solution.py:66
  94.2 0.3 fusion
  94.6 0.7 copy.21
  95.3 0.0 reduce-scatter.7.cloned.1.call-update
  95.3 0.0 reduce-scatter.5.cloned.1.call-start
  95.4 6.3 %copy.23 = bf16[1,4,1024,512]{2,3,1,0:T(8,128)(2,1)} copy(bf16[1,4,1024,512]{3,2,1,0:T(8,128)(2,1)} %get-tuple-element.6) | data formatting | bytes 8388608
  101.7 4.1 %fusion.2 = f32[4,4,16,128]{3,2,1,0:T(8,128)} fusion(bf16[4,1024,4,128]{1,3,2,0:T(8,128)(2,1)} %bitcast.29, f32[4,4,16,1024]{3,2,1,0:T(8,128)S(1)} %get-tuple-element.18, f32[4,4,16]{2,1,0:T(4,128)S(1)} %get-tuple-element.12, pred[4,1024]{1,0:T(4,128)(4,1)S(1)} %broadcast_compare_fusion), kind=kOutput, calls=%fused_computation.5 | convolution fusion | flops 67895296 | bytes 5379072 | tf_op jit(solution)/shard_map/rgqp,rpgd->rgqd/dot_general | solution.py:74
  105.8 0.0 reduce-scatter.5.cloned.1.call-update
  105.8 0.1 reshape.132
  105.9 0.1 fusion.13
  106.0 5.7 %reduce-scatter.7.cloned.1.call-done = f32[16,4]{1,0:T(8,128)} async-done(((f32[64,4]{1,0:T(8,128)}), f32[16,4]{1,0:T(8,128)}) %reduce-scatter.7.cloned.1.call-update) | async-done | bytes 272
  111.7 0.8 copy.20
  112.4 0.1 dynamic-slice_add_fusion
  112.5 18.9 %reduce-scatter.5.cloned.1.call-done = f32[4,16,128]{2,1,0:T(8,128)} async-done(((f32[4,64,128]{2,1,0:T(8,128)}), f32[4,16,128]{2,1,0:T(8,128)}) %reduce-scatter.5.cloned.1.call-update) | async-done | bytes 32784 | tf_op jit(solution)/shard_map/reduce_scatter | solution.py:84
  131.4 0.8 divide_convert_fusion
  132.3 5.2 %all-gather.1 = bf16[4,4,2048]{2,1,0:T(4,128)(2,1)S(1)} all-gather(bf16[1,4,2048]{2,1,0:T(4,128)(2,1)S(1)} %reshape.143), channel_id=1, replica_groups=mesh['groups'=2,'ffn'=4,'width'=2,'sub'=2] {'width','sub'}, dimensions={0}, use_global_device_ids=true | all-gather | bytes 81920 | tf_op jit(solution)/shard_map/all_gather | solution.py:100
  137.6 8.0 %fusion.20 = f32[16,4096]{1,0:T(8,128)S(1)} fusion(bf16[16,2048]{1,0:T(8,128)(2,1)S(1)} %reshape.144, bf16[2048,4096]{1,0:T(8,128)(2,1)} %param.9), kind=kOutput, calls=%fused_computation.46 | convolution fusion | flops 268435456 | bytes 17104896 | tf_op jit(solution)/shard_map/dot_general | solution.py:102
  145.6 21.7 %all-reduce.4 = bf16[16,4096]{1,0:T(8,128)(2,1)S(1)} all-reduce(f32[16,4096]{1,0:T(8,128)S(1)} %fusion.20), channel_id=1, replica_groups=mesh['groups'=2,'ffn'=4,'width'=2,'sub'=2] {'ffn'}, use_global_device_ids=true, to_apply=%region_8.9 | all-reduce | flops 65536 | bytes 393216 | tf_op jit(solution)/shard_map/psum | solution.py:103
  167.3 0.6 dynamic-slice_convert_fusion
  (15 shorter events, 0.2 us)
Async XLA Ops:
  6.5 105.1 %reduce-scatter.7.cloned.1.call-start = ((), (), s32[]{:S(2)}) async-start(), calls=%async_computation.3 | async-start | bytes 40960
  31.0 20.9 %copy-start.1 = (u32[32]{0:T(128)S(1)}, u32[32]{0:T(128)}, u32[]{:S(2)}) copy-start(u32[32]{0:T(128)} %constant.42) | copy-start | bytes 388
  66.4 5.7 %copy-start = (s32[4]{0:T(128)S(1)}, s32[4]{0:T(128)}, u32[]{:S(2)}) copy-start(s32[4]{0:T(128)} %param.11) | copy-start | bytes 52
  95.3 36.1 %reduce-scatter.5.cloned.1.call-start = ((), (), s32[]{:S(2)}) async-start(), calls=%async_computation.2 | async-start | bytes 163840 | tf_op jit(solution)/shard_map/reduce_scatter | solution.py:84
Sparse Core Ops, SparseCore 0:
  95.4 16.1 reduce-scatter.6
  114.0 17.3 reduce-scatter.4
where the time goes:
time: 176 us; the launch traced here: 175 us
  blocking collectives  86 us (49%)
  waiting for transfers between devices  24.6 us (14%)
  matrix products  24.2 us (14%)
  local copies, waits for them, and re-layouts  21.3 us (12%)
  between operations  14.2 us (8%)
  other arithmetic  4.3 us (2%)
    psum x1, blocking collectives, local(): summed_all = lax.psum(partial_all, 'ffn')  21.7 us
    reduce_scatter x1, waiting for transfers between devices, local(): lax.psum_scatter(weighted, 'ffn', scatter_dimension=1, tiled=True)  18.9 us
    unnamed x13, local copies, waits for them, and re-layouts  14.9 us
    all_gather x1, blocking collectives, local(): gathered = lax.all_gather(normed, 'ffn', axis=0, tiled=True)  13.6 us
    all_gather x1, blocking collectives, local(): qkv = lax.all_gather(qkv_part, 'ffn', axis=1, tiled=True)  13.2 us
    pmax x1, blocking collectives, local(): overall_top = lax.pmax(block_top, 'ffn')  12 us
    unnamed x1, blocking collectives  12 us
    dot_general x1, matrix products, local(): jnp.dot(gathered, w_qkv, preferred_element_type=jnp.float32)  8.91 us
  transfers between devices with their start and end apart: 2, of which 2 were waited for; matrix products, arithmetic and copies ran while one was open for 7% of the time, Pallas kernels for 0%

commit v1 on v0

v1 whole, which is shorter than its diff:
```python
import functools
import math

import jax
import jax.numpy as jnp
import numpy as np
from jax import lax
from jax.experimental import pallas as pl
from jax.experimental.pallas import tpu as pltpu
from jax.sharding import PartitionSpec as P

HQ = 64
KVH = 4
DH = 128
GROUP = HQ // KVH
EPS = 1e-05
LOWEST = -1e30
FLOOR = -1e29
EXP2_SCALE = math.log2(math.e) / math.sqrt(DH)
ROWS_AXES = ("width", "sub")
F32 = jnp.float32
BF16 = jnp.bfloat16
VMEM = pl.BlockSpec(memory_space=pltpu.VMEM)
SMEM = pl.BlockSpec(memory_space=pltpu.SMEM)


def three_parts(value):
    high = value.astype(BF16).astype(F32)
    rest = value - high
    middle = rest.astype(BF16).astype(F32)
    return high, middle, rest - middle


def exchange(pieces, axes, count):
    return [pieces[0]] + [
        lax.ppermute(pieces[j], axes, [(i, i ^ j) for i in range(count)])
        for j in range(1, count)
    ]


def column_tile(columns):
    return 256 if columns % 256 == 0 else columns


def rope_kernel(lengths_ref, frequency_ref, cosine_ref, sine_ref):
    rows = cosine_ref.shape[0]
    row = lax.broadcasted_iota(jnp.int32, (rows, DH), 0)
    lane = lax.broadcasted_iota(jnp.int32, (rows, DH), 1)
    position = jnp.zeros((rows, DH), jnp.int32)
    for r in range(rows):
        position = jnp.where(row == r, lengths_ref[r], position)
    angle = position.astype(F32) * frequency_ref[...]
    sine = jnp.sin(angle)
    cosine_ref[...] = jnp.cos(angle)
    sine_ref[...] = jnp.where(lane < DH // 2, -sine, sine)


def project_kernel(n_f, n_w, *refs):
    slots, (gain_ref, w_ref), outs = refs[:n_f], refs[n_f : n_f + 2], refs[n_f + 2 : n_f + 2 + n_w]
    lhs, result = refs[n_f + 2 + n_w :]
    rows = slots[0].shape[0]
    total = n_f * rows
    columns = w_ref.shape[1]
    widened = jnp.concatenate([slot[...].astype(F32) for slot in slots], axis=0)
    squares = jnp.sum(widened * widened, axis=1, keepdims=True)
    scaled = widened * gain_ref[...].astype(F32)
    high = scaled.astype(BF16)
    lhs[:total] = high
    lhs[total:] = (scaled - high.astype(F32)).astype(BF16)
    lane = lax.broadcasted_iota(jnp.int32, (total, 128), 1)
    stats = jnp.zeros((total, 128), F32)
    for at, part in enumerate(three_parts(squares)):
        stats = jnp.where(lane == at, part, stats)
    for k in range(n_f):
        result[k, :, :128] = stats[k * rows : (k + 1) * rows]
    tile = column_tile(columns)

    def step(at, carry):
        start = at * tile
        product = jnp.dot(lhs[...], w_ref[:, pl.ds(pl.multiple_of(start, tile), tile)], preferred_element_type=F32)
        product = product[:total] + product[total:]
        where = pl.ds(pl.multiple_of(start + 128, 128), tile)
        for k in range(n_f):
            result[k, :, where] = product[k * rows : (k + 1) * rows]
        return carry

    if columns == tile:
        product = jnp.dot(lhs[...], w_ref[...], preferred_element_type=F32)
        product = product[:total] + product[total:]
        for k in range(n_f):
            result[k, :, 128:] = product[k * rows : (k + 1) * rows]
    else:
        lax.fori_loop(0, columns // tile, step, 0)
    mine = jnp.bitwise_xor(lax.axis_index("ffn"), lax.axis_index(ROWS_AXES))
    for j in range(n_w):
        outs[j][...] = result[jnp.bitwise_xor(mine, j)].astype(BF16)


def normalise_kernel(features, *refs):
    parts, out = refs[:-1], refs[-1]
    total = parts[0][...].astype(F32)
    for part in parts[1:]:
        total = total + part[...].astype(F32)
    squares = jnp.sum(total[:, :128], axis=1, keepdims=True)
    inverse_rms = 1.0 / jnp.sqrt(squares / features + EPS)
    out[...] = (total[:, 128:] * inverse_rms).astype(BF16)


def attend_kernel(n_f, *refs):
    slots = refs[:n_f]
    cosine_ref, sine_ref, lengths_ref, cache_ref = refs[n_f : n_f + 4]
    outs = refs[n_f + 4 : 2 * n_f + 4]
    shards, heads, results = refs[2 * n_f + 4 :]
    rows, columns = slots[0].shape
    block = cache_ref.shape[2]
    per = HQ // n_f
    f = lax.axis_index("ffn")
    for k in range(n_f):
        shards[jnp.bitwise_xor(f, k)] = slots[k][...].astype(F32)
    for h in range(HQ + 2 * KVH):
        at, end, found = h * DH, (h + 1) * DH, []
        while at < end:
            b, offset = divmod(at, columns)
            length = min(end - at, columns - offset)
            found.append(shards[b, :, offset : offset + length])
            at += length
        heads[:, h, :] = found[0] if len(found) == 1 else jnp.concatenate(found, axis=1)
    lane = lax.broadcasted_iota(jnp.int32, (HQ, 128), 1)
    stats = jnp.zeros((HQ, 128), F32)
    position = f * block + lax.broadcasted_iota(jnp.int32, (1, block), 1)
    for r in range(rows):
        turn_c, turn_s = cosine_ref[r : r + 1, :], sine_ref[r : r + 1, :]

        def rotate(values):
            return (values * turn_c + pltpu.roll(values, DH // 2, 1) * turn_s).astype(BF16)

        queries = rotate(heads[r, :HQ, :])
        joined = heads[r, HQ:, :]
        new_keys = rotate(joined).astype(F32)
        new_values = joined[KVH:]
        empty = jnp.zeros((GROUP, DH), BF16)
        spread = jnp.concatenate(
            [
                jnp.concatenate(
                    [queries[g * GROUP : (g + 1) * GROUP] if c == g else empty for c in range(KVH)], axis=1
                )
                for g in range(KVH)
            ],
            axis=0,
        )
        scores = lax.dot_general(
            spread, cache_ref[0, r], (((1,), (1,)), ((), ())), preferred_element_type=F32
        )
        scores = jnp.where(position < lengths_ref[r], scores, LOWEST)
        keys_wide = jnp.concatenate(
            [jnp.broadcast_to(new_keys[g : g + 1], (GROUP, DH)) for g in range(KVH)], axis=0
        )
        values_wide = jnp.concatenate(
            [jnp.broadcast_to(new_values[g : g + 1], (GROUP, DH)) for g in range(KVH)], axis=0
        )
        own = jnp.sum(queries.astype(F32) * keys_wide, axis=1, keepdims=True)
        own = jnp.where(f == 0, own, LOWEST)
        top = jnp.maximum(jnp.maximum(jnp.max(scores, axis=1, keepdims=True), own), FLOOR)
        probs = jnp.exp2((scores - top) * EXP2_SCALE)
        own_probs = jnp.exp2((own - top) * EXP2_SCALE)
        totals = jnp.sum(probs, axis=1, keepdims=True) + own_probs
        weighted = jnp.dot(probs.astype(BF16), cache_ref[1, r], preferred_element_type=F32)
        weighted = jnp.concatenate(
            [weighted[g * GROUP : (g + 1) * GROUP, g * DH : (g + 1) * DH] for g in range(KVH)], axis=0
        )
        weighted = weighted + own_probs.astype(BF16).astype(F32) * values_wide
        for b in range(n_f):
            results[b, r] = weighted[b * per : (b + 1) * per]
        for at, part in enumerate(three_parts(top) + three_parts(totals)):
            stats = jnp.where(lane == 8 * r + at, part, stats)
    for b in range(n_f):
        results[b, rows] = stats[b * per : (b + 1) * per]
    for j in range(n_f):
        outs[j][...] = results[jnp.bitwise_xor(f, j)].astype(BF16)


def combine_kernel(*refs):
    parts, out = refs[:-1], refs[-1]
    rows = out.shape[0]
    for r in range(rows):
        tops, totals = [], []
        for part in parts:
            stats = part[rows].astype(F32)
            at = 8 * r
            tops.append(stats[:, at : at + 1] + stats[:, at + 1 : at + 2] + stats[:, at + 2 : at + 3])
            totals.append(stats[:, at + 3 : at + 4] + stats[:, at + 4 : at + 5] + stats[:, at + 5 : at + 6])
        top = functools.reduce(jnp.maximum, tops)
        weighted, total = 0.0, 0.0
        for k, part in enumerate(parts):
            share = jnp.exp2((tops[k] - top) * EXP2_SCALE)
            weighted = weighted + share * part[r].astype(F32)
            total = total + share * totals[k]
        out[r] = (weighted / total).astype(BF16)


def output_kernel(n_f, n_w, *refs):
    slots, w_ref, outs = refs[:n_w], refs[n_w], refs[n_w + 1 : n_w + 1 + n_f]
    wide, lhs, result = refs[n_w + 1 + n_f :]
    rows, per, _ = slots[0].shape
    columns = w_ref.shape[1]
    for j in range(n_w):
        wide[j * rows : (j + 1) * rows] = slots[j][...].astype(F32)
    for h in range(per):
        lhs[:, h * DH : (h + 1) * DH] = wide[:, h, :].astype(BF16)
    tile = column_tile(columns)

    def step(at, carry):
        where = pl.ds(pl.multiple_of(at * tile, tile), tile)
        product = jnp.dot(lhs[...], w_ref[:, where], preferred_element_type=F32)
        for j in range(n_w):
            result[j, :, where] = product[j * rows : (j + 1) * rows]
        return carry

    lax.fori_loop(0, columns // tile, step, 0)
    mine = jnp.bitwise_xor(lax.axis_index("ffn"), lax.axis_index(ROWS_AXES))
    for j in range(n_f):
        outs[j][...] = result[jnp.bitwise_xor(mine, j)].astype(BF16)


def sum_kernel(*refs):
    total = refs[0][...].astype(F32)
    for part in refs[1:-1]:
        total = total + part[...].astype(F32)
    refs[-1][...] = total.astype(BF16)


def call(kernel, outs, inputs, name, scratch=(), smem=(), limit=4):
    many = isinstance(outs, list)
    return pl.pallas_call(
        kernel,
        out_shape=outs,
        in_specs=[SMEM if at in smem else VMEM for at in range(len(inputs))],
        out_specs=[VMEM] * len(outs) if many else VMEM,
        scratch_shapes=list(scratch),
        compiler_params=pltpu.CompilerParams(vmem_limit_bytes=limit << 20),
        name=name,
    )(*inputs)


def local(n_f, n_w, tokens, norm_gain, w_qkv, w_out, kv_cache, lengths):
    rows, features = tokens.shape
    columns, out_columns = w_qkv.shape[1], w_out.shape[1]
    per = HQ // n_f
    shape = jax.ShapeDtypeStruct
    w_qkv = pltpu.with_memory_space_constraint(w_qkv, pltpu.VMEM)
    w_out = pltpu.with_memory_space_constraint(w_out, pltpu.VMEM)
    kv_cache = pltpu.with_memory_space_constraint(kv_cache, pltpu.VMEM)
    half = 500000.0 ** (-(np.arange(DH // 2, dtype=np.float64) * 2.0 / DH))
    frequency = jnp.asarray(np.concatenate([half, half])[None, :], F32)

    token_slots = exchange([tokens] * n_f, "ffn", n_f)
    cosine, sine = call(
        rope_kernel, [shape((rows, DH), F32)] * 2, [lengths, frequency], "rope", smem=(0,)
    )
    projected = call(
        functools.partial(project_kernel, n_f, n_w),
        [shape((rows, 128 + columns), BF16)] * n_w,
        token_slots + [norm_gain.reshape(1, features), w_qkv],
        "project",
        scratch=[
            pltpu.VMEM((2 * n_f * rows, features), BF16),
            pltpu.VMEM((n_f, rows, 128 + columns), F32),
        ],
    )
    partials = exchange(projected, ROWS_AXES, n_w)
    qkv = call(
        functools.partial(normalise_kernel, float(features * n_w)),
        shape((rows, columns), BF16),
        partials,
        "normalise",
    )
    qkv_slots = exchange([qkv] * n_f, "ffn", n_f)
    attended = call(
        functools.partial(attend_kernel, n_f),
        [shape((rows + 1, per, DH), BF16)] * n_f,
        qkv_slots + [cosine, sine, lengths, kv_cache],
        "attend",
        scratch=[
            pltpu.VMEM((n_f, rows, columns), F32),
            pltpu.VMEM((rows, HQ + 2 * KVH, DH), F32),
            pltpu.VMEM((n_f, rows + 1, per, DH), F32),
        ],
        smem=(n_f + 2,),
    )
    attention = call(
        combine_kernel,
        shape((rows, per, DH), BF16),
        exchange(attended, "ffn", n_f),
        "combine",
    )
    row_slots = exchange([attention] * n_w, ROWS_AXES, n_w)
    summands = call(
        functools.partial(output_kernel, n_f, n_w),
        [shape((rows, out_columns), BF16)] * n_f,
        row_slots + [w_out],
        "output",
        scratch=[
            pltpu.VMEM((n_w * rows, per, DH), F32),
            pltpu.VMEM((n_w * rows, per * DH), BF16),
            pltpu.VMEM((n_w, rows, out_columns), F32),
        ],
    )
    return call(
        sum_kernel, shape((rows, out_columns), BF16), exchange(summands, "ffn", n_f), "total"
    )


def solution(mesh):
    placed = (
        P(("groups", "ffn"), ("width", "sub")),
        P(("width", "sub")),
        P(("width", "sub"), "ffn"),
        P("ffn", ("width", "sub")),
        P(None, ("groups", "width", "sub"), "ffn", None),
        P(("groups", "width", "sub")),
    )
    n_f, n_w = mesh.shape["ffn"], mesh.shape["width"] * mesh.shape["sub"]
    assert n_f == n_w and n_f & (n_f - 1) == 0
    return jax.shard_map(
        functools.partial(local, n_f, n_w),
        mesh=mesh,
        in_specs=placed,
        out_specs=P(("groups", "ffn"), ("width", "sub")),
        check_vma=False,
    )
```

time: 176 us -> 66.8 us (0.38)
  blocking collectives: 86 us -> 0 us
  matrix products: 24.2 us -> 0 us
  starting transfers between devices: 0.04 us -> 22.9 us
  between operations: 14.2 us -> 0.09 us
  Pallas kernels: 0 us -> 13.6 us
  local copies, waits for them, and re-layouts: 21.3 us -> 11.2 us
  waiting for transfers between devices: 24.6 us -> 18.7 us
  other arithmetic: 4.3 us -> 0 us
    all_gather x3 -> x0, blocking collectives: 32 us -> none  [the longest x1 13.6 us: local(): gathered = lax.all_gather(normed, 'ffn', axis=0, tiled=True)]
    psum x2 -> x0, blocking collectives: 30 us -> none  [the longest x1 21.7 us: local(): summed_all = lax.psum(partial_all, 'ffn')]
    dot_general x5 -> x0, matrix products: 24.2 us -> none  [the longest x1 8.91 us: local(): jnp.dot(gathered, w_qkv, preferred_element_type=jnp.float32)]
    ppermute x0 -> x18, starting transfers between devices: none -> 22.9 us  [exchange(): lax.ppermute(pieces[j], axes, [(i, i ^ j) for i in range(count)])]
    reduce_scatter x1 -> x0, waiting for transfers between devices: 18.9 us -> none  [local(): lax.psum_scatter(weighted, 'ffn', scatter_dimension=1, tiled=True)]
    ppermute x0 -> x18, waiting for transfers between devices: none -> 18.7 us  [exchange(): lax.ppermute(pieces[j], axes, [(i, i ^ j) for i in range(count)])]
    pallas_call x0 -> x7, Pallas kernels: none -> 13.6 us  [call(): pl.pallas_call(kernel, out_shape=outs, in_specs=[SMEM if at in smem else...]
    pmax x1 -> x0, blocking collectives: 12 us -> none  [local(): overall_top = lax.pmax(block_top, 'ffn')]
  transfers between devices with their start and end apart: 2 -> 18, of which waited for: 2 -> 13; matrix products, arithmetic and copies ran while one was open for 7% -> 1% of each run, Pallas kernels for 0% -> 1%
where the time goes in v1:
time: 66.8 us; the launch traced here: 66.5 us
  starting transfers between devices  22.9 us (34%)
  waiting for transfers between devices  18.7 us (28%)
  Pallas kernels  13.6 us (20%)
  local copies, waits for them, and re-layouts  11.2 us (17%)
    ppermute x18, starting transfers between devices, exchange(): lax.ppermute(pieces[j], axes, [(i, i ^ j) for i in range(count)])  22.9 us
    ppermute x18, waiting for transfers between devices, exchange(): lax.ppermute(pieces[j], axes, [(i, i ^ j) for i in range(count)])  18.7 us
    pallas_call x7, Pallas kernels, call(): pl.pallas_call(kernel, out_shape=outs, in_specs=[SMEM if at in smem else...  13.6 us
    unnamed x12, local copies, waits for them, and re-layouts  10.5 us
  transfers between devices with their start and end apart: 18, of which 13 were waited for; matrix products, arithmetic and copies ran while one was open for 1% of the time, Pallas kernels for 1%

profile of v1, /device:TPU:0, one launch (start us, length us, event | category | flops | bytes accessed | tf_op | source)
XLA Modules:
  0.0 66.5 jit_solution(9910392568853586039)
XLA Ops:
  0.0 0.0 copy-start.5
  0.0 0.0 copy-start.4
  0.0 4.0 %collective-permute-start.1 = (bf16[4,4096]{1,0:T(4,128)(2,1)}, bf16[4,4096]{1,0:T(4,128)(2,1)S(1)}, u32[]{:S(2)}, u32[]{:S(2)}) collective-permute-start(bf16[4,4096]{1,0:T(4,128)(2,1)} %refs_0_.1), channel_id=1, source_target_pairs={{0,8},{4,12},{8,0},{12,4},{1,9},{5,13},{9,1},{13,5},{2,10},{6,14},... | collective-permute-start | bytes 98312 | tf_op jit(solution)/shard_map/ppermute | solution.py:36
  4.0 1.6 %collective-permute-start = (bf16[4,4096]{1,0:T(4,128)(2,1)}, bf16[4,4096]{1,0:T(4,128)(2,1)S(1)}, u32[]{:S(2)}, u32[]{:S(2)}) collective-permute-start(bf16[4,4096]{1,0:T(4,128)(2,1)} %refs_0_.1), channel_id=1, source_target_pairs={{0,4},{4,0},{8,12},{12,8},{1,5},{5,1},{9,13},{13,9},{2,6},{6,2},{1... | collective-permute-start | bytes 98312 | tf_op jit(solution)/shard_map/ppermute | solution.py:36
  5.6 0.0 collective-permute-start.2
  5.6 0.7 %reshape.3.refs_4_ = bf16[1,4096]{1,0:T(2,128)(2,1)S(1)} reshape(bf16[4096]{0:T(1024)(128)(2,1)} %param.8) | data formatting | bytes 16384 | tf_op jit(solution)/shard_map/reshape | solution.py:263
  6.3 0.3 collective-permute-done.1.refs_2_
  6.6 1.6 %collective-permute-done.refs_1_ = bf16[4,4096]{1,0:T(4,128)(2,1)S(1)} collective-permute-done((bf16[4,4096]{1,0:T(4,128)(2,1)}, bf16[4,4096]{1,0:T(4,128)(2,1)S(1)}, u32[]{:S(2)}, u32[]{:S(2)}) %collective-permute-start) | collective-permute-done | bytes 32800 | tf_op jit(solution)/shard_map/ppermute | solution.py:36
  8.2 3.4 %collective-permute-done.2.refs_3_ = bf16[4,4096]{1,0:T(4,128)(2,1)S(1)} collective-permute-done((bf16[4,4096]{1,0:T(4,128)(2,1)}, bf16[4,4096]{1,0:T(4,128)(2,1)S(1)}, u32[]{:S(2)}, u32[]{:S(2)}) %collective-permute-start.2) | collective-permute-done | bytes 32800 | tf_op jit(solution)/shard_map/ppermute | solution.py:36
  11.5 0.0 copy-start
  11.5 6.4 %copy-done = bf16[4096,2304]{1,0:T(8,128)(2,1)S(1)} copy-done((bf16[4096,2304]{1,0:T(8,128)(2,1)S(1)}, bf16[4096,2304]{1,0:T(8,128)(2,1)}, u32[]{:S(2)}) %copy-start) | copy-done | bytes 18874392
  17.9 0.0 copy-start.3
  17.9 0.8 %copy-done.3 = bf16[4,4096]{1,0:T(4,128)(2,1)S(1)} copy-done((bf16[4,4096]{1,0:T(4,128)(2,1)S(1)}, bf16[4,4096]{1,0:T(4,128)(2,1)}, u32[]{:S(2)}) %copy-start.3) | copy-done | bytes 32792
  18.7 0.0 copy-start.1
  18.7 4.2 %project.1 = (bf16[4,2432]{1,0:T(4,128)(2,1)S(1)}, bf16[4,2432]{1,0:T(4,128)(2,1)S(1)}, bf16[4,2432]{1,0:T(4,128)(2,1)S(1)}, bf16[4,2432]{1,0:T(4,128)(2,1)S(1)}) custom-call(bf16[4,4096]{1,0:T(4,128)(2,1)S(1)} %copy-done.3, bf16[4,4096]{1,0:T(4,128)(2,1)S(1)} %collective-permute-done.refs_1_, bf16[4,4096]{1,0:T(4,128)(2,1)S(1)} %collective-permute-done.1.refs_2_, ...), custom_call_target="tpu_custom_call" | custom-call | tf_op jit(solution)/shard_map/project/pallas_call | solution.py:234
  22.9 0.1 collective-permute-start.3
  23.0 1.6 %collective-permute-start.4 = (bf16[4,2432]{1,0:T(4,128)(2,1)S(1)}, bf16[4,2432]{1,0:T(4,128)(2,1)S(1)}, u32[]{:S(2)}, u32[]{:S(2)}) collective-permute-start(bf16[4,2432]{1,0:T(4,128)(2,1)S(1)} %get-tuple-element.21), channel_id=1, source_target_pairs={{0,2},{1,3},{2,0},{3,1},{4,6},{5,7},{6,4},{7,5},{8,10},{9,11},{10,... | collective-permute-start | bytes 58376 | tf_op jit(solution)/shard_map/ppermute | solution.py:36
  24.5 0.3 collective-permute-start.5
  24.8 0.0 collective-permute-done.3.refs_1_
  24.8 2.0 %collective-permute-done.4.refs_2_ = bf16[4,2432]{1,0:T(4,128)(2,1)S(1)} collective-permute-done((bf16[4,2432]{1,0:T(4,128)(2,1)S(1)}, bf16[4,2432]{1,0:T(4,128)(2,1)S(1)}, u32[]{:S(2)}, u32[]{:S(2)}) %collective-permute-start.4) | collective-permute-done | bytes 19488 | tf_op jit(solution)/shard_map/ppermute | solution.py:36
  26.8 0.9 %collective-permute-done.5.refs_3_ = bf16[4,2432]{1,0:T(4,128)(2,1)S(1)} collective-permute-done((bf16[4,2432]{1,0:T(4,128)(2,1)S(1)}, bf16[4,2432]{1,0:T(4,128)(2,1)S(1)}, u32[]{:S(2)}, u32[]{:S(2)}) %collective-permute-start.5) | collective-permute-done | bytes 19488 | tf_op jit(solution)/shard_map/ppermute | solution.py:36
  27.7 0.1 normalise.1.refs_0_
  27.8 0.4 collective-permute-start.8
  28.2 0.1 collective-permute-start.7
  28.4 3.9 %collective-permute-start.6 = (bf16[4,2304]{1,0:T(4,128)(2,1)S(1)}, bf16[4,2304]{1,0:T(4,128)(2,1)S(1)}, u32[]{:S(2)}, u32[]{:S(2)}) collective-permute-start(bf16[4,2304]{1,0:T(4,128)(2,1)S(1)} %normalise.1.refs_0_), channel_id=1, source_target_pairs={{0,4},{4,0},{8,12},{12,8},{1,5},{5,1},{9,13},{13,9},{2,6},{6,2},{1... | collective-permute-start | bytes 55304 | tf_op jit(solution)/shard_map/ppermute | solution.py:36
  32.3 0.0 copy-done.5
  32.3 0.0 copy-done.4
  32.3 0.6 rope.1
  32.9 0.6 collective-permute-done.8.refs_3_
  33.5 0.0 collective-permute-done.7.refs_2_
  33.5 0.6 collective-permute-done.6.refs_1_
  34.0 0.0 copy-start.2
  34.0 3.4 %copy-done.2 = bf16[2,4,1024,512]{3,2,1,0:T(8,128)(2,1)S(1)} copy-done((bf16[2,4,1024,512]{3,2,1,0:T(8,128)(2,1)S(1)}, bf16[2,4,1024,512]{3,2,1,0:T(8,128)(2,1)}, u32[]{:S(2)}) %copy-start.2) | copy-done | bytes 8388632
  37.4 3.5 %attend.1 = (bf16[5,16,128]{2,1,0:T(8,128)(2,1)S(1)}, bf16[5,16,128]{2,1,0:T(8,128)(2,1)S(1)}, bf16[5,16,128]{2,1,0:T(8,128)(2,1)S(1)}, bf16[5,16,128]{2,1,0:T(8,128)(2,1)S(1)}) custom-call(bf16[4,2304]{1,0:T(4,128)(2,1)S(1)} %normalise.1.refs_0_, bf16[4,2304]{1,0:T(4,128)(2,1)S(1)} %collective-permute-done.6.refs_1_, ...), custom_call_target="tpu_custom_call" | custom-call | tf_op jit(solution)/shard_map/attend/pallas_call | solution.py:234
  40.9 2.1 %collective-permute-start.9 = (bf16[5,16,128]{2,1,0:T(8,128)(2,1)S(1)}, bf16[5,16,128]{2,1,0:T(8,128)(2,1)S(1)}, u32[]{:S(2)}, u32[]{:S(2)}) collective-permute-start(bf16[5,16,128]{2,1,0:T(8,128)(2,1)S(1)} %get-tuple-element.26), channel_id=1, source_target_pairs={{0,4},{4,0},{8,12},{12,8},{1,5},{5,1},{9,13},{13,9},{2,6},{6,2},{1... | collective-permute-start | bytes 61448 | tf_op jit(solution)/shard_map/ppermute | solution.py:36
  43.0 0.9 %collective-permute-start.10 = (bf16[5,16,128]{2,1,0:T(8,128)(2,1)S(1)}, bf16[5,16,128]{2,1,0:T(8,128)(2,1)S(1)}, u32[]{:S(2)}, u32[]{:S(2)}) collective-permute-start(bf16[5,16,128]{2,1,0:T(8,128)(2,1)S(1)} %get-tuple-element.27), channel_id=1, source_target_pairs={{0,8},{4,12},{8,0},{12,4},{1,9},{5,13},{9,1},{13,5},{2,10},{6,14},... | collective-permute-start | bytes 61448 | tf_op jit(solution)/shard_map/ppermute | solution.py:36
  43.9 1.5 %collective-permute-start.11 = (bf16[5,16,128]{2,1,0:T(8,128)(2,1)S(1)}, bf16[5,16,128]{2,1,0:T(8,128)(2,1)S(1)}, u32[]{:S(2)}, u32[]{:S(2)}) collective-permute-start(bf16[5,16,128]{2,1,0:T(8,128)(2,1)S(1)} %get-tuple-element.28), channel_id=1, source_target_pairs={{0,12},{4,8},{8,4},{12,0},{1,13},{5,9},{9,5},{13,1},{2,14},{6,10},... | collective-permute-start | bytes 61448 | tf_op jit(solution)/shard_map/ppermute | solution.py:36
  45.4 0.0 collective-permute-done.9.refs_1_
  45.5 2.2 %collective-permute-done.10.refs_2_ = bf16[5,16,128]{2,1,0:T(8,128)(2,1)S(1)} collective-permute-done((bf16[5,16,128]{2,1,0:T(8,128)(2,1)S(1)}, bf16[5,16,128]{2,1,0:T(8,128)(2,1)S(1)}, u32[]{:S(2)}, u32[]{:S(2)}) %collective-permute-start.10) | collective-permute-done | bytes 20512 | tf_op jit(solution)/shard_map/ppermute | solution.py:36
  47.7 1.8 %collective-permute-done.11.refs_3_ = bf16[5,16,128]{2,1,0:T(8,128)(2,1)S(1)} collective-permute-done((bf16[5,16,128]{2,1,0:T(8,128)(2,1)S(1)}, bf16[5,16,128]{2,1,0:T(8,128)(2,1)S(1)}, u32[]{:S(2)}, u32[]{:S(2)}) %collective-permute-start.11) | collective-permute-done | bytes 20512 | tf_op jit(solution)/shard_map/ppermute | solution.py:36
  49.5 0.3 combine.1.refs_0_
  49.8 0.1 collective-permute-start.14
  49.8 0.8 %collective-permute-start.13 = (bf16[4,16,128]{2,1,0:T(8,128)(2,1)S(1)}, bf16[4,16,128]{2,1,0:T(8,128)(2,1)S(1)}, u32[]{:S(2)}, u32[]{:S(2)}) collective-permute-start(bf16[4,16,128]{2,1,0:T(8,128)(2,1)S(1)} %combine.1.refs_0_), channel_id=1, source_target_pairs={{0,2},{1,3},{2,0},{3,1},{4,6},{5,7},{6,4},{7,5},{8,10},{9,11},{10,... | collective-permute-start | bytes 49160 | tf_op jit(solution)/shard_map/ppermute | solution.py:36
  50.6 1.0 %collective-permute-start.12 = (bf16[4,16,128]{2,1,0:T(8,128)(2,1)S(1)}, bf16[4,16,128]{2,1,0:T(8,128)(2,1)S(1)}, u32[]{:S(2)}, u32[]{:S(2)}) collective-permute-start(bf16[4,16,128]{2,1,0:T(8,128)(2,1)S(1)} %combine.1.refs_0_), channel_id=1, source_target_pairs={{0,1},{1,0},{2,3},{3,2},{4,5},{5,4},{6,7},{7,6},{8,9},{9,8},{10,11... | collective-permute-start | bytes 49160 | tf_op jit(solution)/shard_map/ppermute | solution.py:36
  51.7 1.3 %collective-permute-done.14.refs_3_ = bf16[4,16,128]{2,1,0:T(8,128)(2,1)S(1)} collective-permute-done((bf16[4,16,128]{2,1,0:T(8,128)(2,1)S(1)}, bf16[4,16,128]{2,1,0:T(8,128)(2,1)S(1)}, u32[]{:S(2)}, u32[]{:S(2)}) %collective-permute-start.14) | collective-permute-done | bytes 16416 | tf_op jit(solution)/shard_map/ppermute | solution.py:36
  53.0 0.7 collective-permute-done.13.refs_2_
  53.6 0.0 collective-permute-done.12.refs_1_
  53.6 0.0 copy-done.1
  53.6 4.3 %output.1 = (bf16[4,4096]{1,0:T(4,128)(2,1)S(1)}, bf16[4,4096]{1,0:T(4,128)(2,1)S(1)}, bf16[4,4096]{1,0:T(4,128)(2,1)S(1)}, bf16[4,4096]{1,0:T(4,128)(2,1)S(1)}) custom-call(bf16[4,16,128]{2,1,0:T(8,128)(2,1)S(1)} %combine.1.refs_0_, bf16[4,16,128]{2,1,0:T(8,128)(2,1)S(1)} %collective-permute-done.12.refs_1_, ...), custom_call_target="tpu_custom_call" | custom-call | tf_op jit(solution)/shard_map/output/pallas_call | solution.py:234
  58.0 0.1 collective-permute-start.15
  58.1 2.1 %collective-permute-start.16 = (bf16[4,4096]{1,0:T(4,128)(2,1)S(1)}, bf16[4,4096]{1,0:T(4,128)(2,1)S(1)}, u32[]{:S(2)}, u32[]{:S(2)}) collective-permute-start(bf16[4,4096]{1,0:T(4,128)(2,1)S(1)} %get-tuple-element.31), channel_id=1, source_target_pairs={{0,8},{4,12},{8,0},{12,4},{1,9},{5,13},{9,1},{13,5},{2,10},{6,14},... | collective-permute-start | bytes 98312 | tf_op jit(solution)/shard_map/ppermute | solution.py:36
  60.1 2.3 %collective-permute-start.17 = (bf16[4,4096]{1,0:T(4,128)(2,1)S(1)}, bf16[4,4096]{1,0:T(4,128)(2,1)S(1)}, u32[]{:S(2)}, u32[]{:S(2)}) collective-permute-start(bf16[4,4096]{1,0:T(4,128)(2,1)S(1)} %get-tuple-element.32), channel_id=1, source_target_pairs={{0,12},{4,8},{8,4},{12,0},{1,13},{5,9},{9,5},{13,1},{2,14},{6,10},... | collective-permute-start | bytes 98312 | tf_op jit(solution)/shard_map/ppermute | solution.py:36
  62.4 0.0 collective-permute-done.15.refs_1_
  62.4 0.6 collective-permute-done.16.refs_2_
  63.1 2.8 %collective-permute-done.17.refs_3_ = bf16[4,4096]{1,0:T(4,128)(2,1)S(1)} collective-permute-done((bf16[4,4096]{1,0:T(4,128)(2,1)S(1)}, bf16[4,4096]{1,0:T(4,128)(2,1)S(1)}, u32[]{:S(2)}, u32[]{:S(2)}) %collective-permute-start.17) | collective-permute-done | bytes 32800 | tf_op jit(solution)/shard_map/ppermute | solution.py:36
  65.9 0.6 total.1
Async XLA Ops:
  0.0 32.3 %copy-start.5 = (f32[1,128]{1,0:T(1,128)S(1)}, f32[1,128]{1,0:T(1,128)}, u32[]{:S(2)}) copy-start(f32[1,128]{1,0:T(1,128)} %constant.2.clone.frequency_ref) | copy-start | bytes 1540
  0.0 32.3 %copy-start.4 = (s32[4]{0:T(128)S(1)}, s32[4]{0:T(128)}, u32[]{:S(2)}) copy-start(s32[4]{0:T(128)} %refs_6_.1) | copy-start | bytes 52
  0.0 6.6 %collective-permute-start.1 = (bf16[4,4096]{1,0:T(4,128)(2,1)}, bf16[4,4096]{1,0:T(4,128)(2,1)S(1)}, u32[]{:S(2)}, u32[]{:S(2)}) collective-permute-start(bf16[4,4096]{1,0:T(4,128)(2,1)} %refs_0_.1), channel_id=1, source_target_pairs={{0,8},{4,12},{8,0},{12,4},{1,9},{5,13},{9,1},{13,5},{2,10},{6,14},... | collective-permute-start | bytes 98312 | tf_op jit(solution)/shard_map/ppermute | solution.py:36
  4.0 4.1 %collective-permute-start = (bf16[4,4096]{1,0:T(4,128)(2,1)}, bf16[4,4096]{1,0:T(4,128)(2,1)S(1)}, u32[]{:S(2)}, u32[]{:S(2)}) collective-permute-start(bf16[4,4096]{1,0:T(4,128)(2,1)} %refs_0_.1), channel_id=1, source_target_pairs={{0,4},{4,0},{8,12},{12,8},{1,5},{5,1},{9,13},{13,9},{2,6},{6,2},{1... | collective-permute-start | bytes 98312 | tf_op jit(solution)/shard_map/ppermute | solution.py:36
  5.6 5.9 %collective-permute-start.2 = (bf16[4,4096]{1,0:T(4,128)(2,1)}, bf16[4,4096]{1,0:T(4,128)(2,1)S(1)}, u32[]{:S(2)}, u32[]{:S(2)}) collective-permute-start(bf16[4,4096]{1,0:T(4,128)(2,1)} %refs_0_.1), channel_id=1, source_target_pairs={{0,12},{4,8},{8,4},{12,0},{1,13},{5,9},{9,5},{13,1},{2,14},{6,10},... | collective-permute-start | bytes 98312 | tf_op jit(solution)/shard_map/ppermute | solution.py:36
  11.5 6.4 %copy-start = (bf16[4096,2304]{1,0:T(8,128)(2,1)S(1)}, bf16[4096,2304]{1,0:T(8,128)(2,1)}, u32[]{:S(2)}) copy-start(bf16[4096,2304]{1,0:T(8,128)(2,1)} %refs_5_.1) | copy-start | bytes 56623108
  17.9 0.8 %copy-start.3 = (bf16[4,4096]{1,0:T(4,128)(2,1)S(1)}, bf16[4,4096]{1,0:T(4,128)(2,1)}, u32[]{:S(2)}) copy-start(bf16[4,4096]{1,0:T(4,128)(2,1)} %refs_0_.1) | copy-start | bytes 98308
  18.7 35.0 %copy-start.1 = (bf16[2048,4096]{1,0:T(8,128)(2,1)S(1)}, bf16[2048,4096]{1,0:T(8,128)(2,1)}, u32[]{:S(2)}) copy-start(bf16[2048,4096]{1,0:T(8,128)(2,1)} %refs_4_.1) | copy-start | bytes 50331652
  22.9 1.9 %collective-permute-start.3 = (bf16[4,2432]{1,0:T(4,128)(2,1)S(1)}, bf16[4,2432]{1,0:T(4,128)(2,1)S(1)}, u32[]{:S(2)}, u32[]{:S(2)}) collective-permute-start(bf16[4,2432]{1,0:T(4,128)(2,1)S(1)} %get-tuple-element.20), channel_id=1, source_target_pairs={{0,1},{1,0},{2,3},{3,2},{4,5},{5,4},{6,7},{7,6},{8,9},{9,8},{10,11... | collective-permute-start | bytes 58376 | tf_op jit(solution)/shard_map/ppermute | solution.py:36
  23.0 3.8 %collective-permute-start.4 = (bf16[4,2432]{1,0:T(4,128)(2,1)S(1)}, bf16[4,2432]{1,0:T(4,128)(2,1)S(1)}, u32[]{:S(2)}, u32[]{:S(2)}) collective-permute-start(bf16[4,2432]{1,0:T(4,128)(2,1)S(1)} %get-tuple-element.21), channel_id=1, source_target_pairs={{0,2},{1,3},{2,0},{3,1},{4,6},{5,7},{6,4},{7,5},{8,10},{9,11},{10,... | collective-permute-start | bytes 58376 | tf_op jit(solution)/shard_map/ppermute | solution.py:36
  24.5 3.2 %collective-permute-start.5 = (bf16[4,2432]{1,0:T(4,128)(2,1)S(1)}, bf16[4,2432]{1,0:T(4,128)(2,1)S(1)}, u32[]{:S(2)}, u32[]{:S(2)}) collective-permute-start(bf16[4,2432]{1,0:T(4,128)(2,1)S(1)} %get-tuple-element.22), channel_id=1, source_target_pairs={{0,3},{1,2},{2,1},{3,0},{4,7},{5,6},{6,5},{7,4},{8,11},{9,10},{10,... | collective-permute-start | bytes 58376 | tf_op jit(solution)/shard_map/ppermute | solution.py:36
  27.8 5.6 %collective-permute-start.8 = (bf16[4,2304]{1,0:T(4,128)(2,1)S(1)}, bf16[4,2304]{1,0:T(4,128)(2,1)S(1)}, u32[]{:S(2)}, u32[]{:S(2)}) collective-permute-start(bf16[4,2304]{1,0:T(4,128)(2,1)S(1)} %normalise.1.refs_0_), channel_id=1, source_target_pairs={{0,12},{4,8},{8,4},{12,0},{1,13},{5,9},{9,5},{13,1},{2,14},{6,10},... | collective-permute-start | bytes 55304 | tf_op jit(solution)/shard_map/ppermute | solution.py:36
  28.2 5.2 %collective-permute-start.7 = (bf16[4,2304]{1,0:T(4,128)(2,1)S(1)}, bf16[4,2304]{1,0:T(4,128)(2,1)S(1)}, u32[]{:S(2)}, u32[]{:S(2)}) collective-permute-start(bf16[4,2304]{1,0:T(4,128)(2,1)S(1)} %normalise.1.refs_0_), channel_id=1, source_target_pairs={{0,8},{4,12},{8,0},{12,4},{1,9},{5,13},{9,1},{13,5},{2,10},{6,14},... | collective-permute-start | bytes 55304 | tf_op jit(solution)/shard_map/ppermute | solution.py:36
  28.4 5.7 %collective-permute-start.6 = (bf16[4,2304]{1,0:T(4,128)(2,1)S(1)}, bf16[4,2304]{1,0:T(4,128)(2,1)S(1)}, u32[]{:S(2)}, u32[]{:S(2)}) collective-permute-start(bf16[4,2304]{1,0:T(4,128)(2,1)S(1)} %normalise.1.refs_0_), channel_id=1, source_target_pairs={{0,4},{4,0},{8,12},{12,8},{1,5},{5,1},{9,13},{13,9},{2,6},{6,2},{1... | collective-permute-start | bytes 55304 | tf_op jit(solution)/shard_map/ppermute | solution.py:36
  34.0 3.4 %copy-start.2 = (bf16[2,4,1024,512]{3,2,1,0:T(8,128)(2,1)S(1)}, bf16[2,4,1024,512]{3,2,1,0:T(8,128)(2,1)}, u32[]{:S(2)}) copy-start(bf16[2,4,1024,512]{3,2,1,0:T(8,128)(2,1)} %refs_7_.1) | copy-start | bytes 25165828
  40.9 4.5 %collective-permute-start.9 = (bf16[5,16,128]{2,1,0:T(8,128)(2,1)S(1)}, bf16[5,16,128]{2,1,0:T(8,128)(2,1)S(1)}, u32[]{:S(2)}, u32[]{:S(2)}) collective-permute-start(bf16[5,16,128]{2,1,0:T(8,128)(2,1)S(1)} %get-tuple-element.26), channel_id=1, source_target_pairs={{0,4},{4,0},{8,12},{12,8},{1,5},{5,1},{9,13},{13,9},{2,6},{6,2},{1... | collective-permute-start | bytes 61448 | tf_op jit(solution)/shard_map/ppermute | solution.py:36
  43.0 4.7 %collective-permute-start.10 = (bf16[5,16,128]{2,1,0:T(8,128)(2,1)S(1)}, bf16[5,16,128]{2,1,0:T(8,128)(2,1)S(1)}, u32[]{:S(2)}, u32[]{:S(2)}) collective-permute-start(bf16[5,16,128]{2,1,0:T(8,128)(2,1)S(1)} %get-tuple-element.27), channel_id=1, source_target_pairs={{0,8},{4,12},{8,0},{12,4},{1,9},{5,13},{9,1},{13,5},{2,10},{6,14},... | collective-permute-start | bytes 61448 | tf_op jit(solution)/shard_map/ppermute | solution.py:36
  43.9 5.6 %collective-permute-start.11 = (bf16[5,16,128]{2,1,0:T(8,128)(2,1)S(1)}, bf16[5,16,128]{2,1,0:T(8,128)(2,1)S(1)}, u32[]{:S(2)}, u32[]{:S(2)}) collective-permute-start(bf16[5,16,128]{2,1,0:T(8,128)(2,1)S(1)} %get-tuple-element.28), channel_id=1, source_target_pairs={{0,12},{4,8},{8,4},{12,0},{1,13},{5,9},{9,5},{13,1},{2,14},{6,10},... | collective-permute-start | bytes 61448 | tf_op jit(solution)/shard_map/ppermute | solution.py:36
  49.8 3.2 %collective-permute-start.14 = (bf16[4,16,128]{2,1,0:T(8,128)(2,1)S(1)}, bf16[4,16,128]{2,1,0:T(8,128)(2,1)S(1)}, u32[]{:S(2)}, u32[]{:S(2)}) collective-permute-start(bf16[4,16,128]{2,1,0:T(8,128)(2,1)S(1)} %combine.1.refs_0_), channel_id=1, source_target_pairs={{0,3},{1,2},{2,1},{3,0},{4,7},{5,6},{6,5},{7,4},{8,11},{9,10},{10,... | collective-permute-start | bytes 49160 | tf_op jit(solution)/shard_map/ppermute | solution.py:36
  49.8 3.8 %collective-permute-start.13 = (bf16[4,16,128]{2,1,0:T(8,128)(2,1)S(1)}, bf16[4,16,128]{2,1,0:T(8,128)(2,1)S(1)}, u32[]{:S(2)}, u32[]{:S(2)}) collective-permute-start(bf16[4,16,128]{2,1,0:T(8,128)(2,1)S(1)} %combine.1.refs_0_), channel_id=1, source_target_pairs={{0,2},{1,3},{2,0},{3,1},{4,6},{5,7},{6,4},{7,5},{8,10},{9,11},{10,... | collective-permute-start | bytes 49160 | tf_op jit(solution)/shard_map/ppermute | solution.py:36
  50.6 3.0 %collective-permute-start.12 = (bf16[4,16,128]{2,1,0:T(8,128)(2,1)S(1)}, bf16[4,16,128]{2,1,0:T(8,128)(2,1)S(1)}, u32[]{:S(2)}, u32[]{:S(2)}) collective-permute-start(bf16[4,16,128]{2,1,0:T(8,128)(2,1)S(1)} %combine.1.refs_0_), channel_id=1, source_target_pairs={{0,1},{1,0},{2,3},{3,2},{4,5},{5,4},{6,7},{7,6},{8,9},{9,8},{10,11... | collective-permute-start | bytes 49160 | tf_op jit(solution)/shard_map/ppermute | solution.py:36
  58.0 4.5 %collective-permute-start.15 = (bf16[4,4096]{1,0:T(4,128)(2,1)S(1)}, bf16[4,4096]{1,0:T(4,128)(2,1)S(1)}, u32[]{:S(2)}, u32[]{:S(2)}) collective-permute-start(bf16[4,4096]{1,0:T(4,128)(2,1)S(1)} %get-tuple-element.30), channel_id=1, source_target_pairs={{0,4},{4,0},{8,12},{12,8},{1,5},{5,1},{9,13},{13,9},{2,6},{6,2},{1... | collective-permute-start | bytes 98312 | tf_op jit(solution)/shard_map/ppermute | solution.py:36
  58.1 5.0 %collective-permute-start.16 = (bf16[4,4096]{1,0:T(4,128)(2,1)S(1)}, bf16[4,4096]{1,0:T(4,128)(2,1)S(1)}, u32[]{:S(2)}, u32[]{:S(2)}) collective-permute-start(bf16[4,4096]{1,0:T(4,128)(2,1)S(1)} %get-tuple-element.31), channel_id=1, source_target_pairs={{0,8},{4,12},{8,0},{12,4},{1,9},{5,13},{9,1},{13,5},{2,10},{6,14},... | collective-permute-start | bytes 98312 | tf_op jit(solution)/shard_map/ppermute | solution.py:36
  60.1 5.7 %collective-permute-start.17 = (bf16[4,4096]{1,0:T(4,128)(2,1)S(1)}, bf16[4,4096]{1,0:T(4,128)(2,1)S(1)}, u32[]{:S(2)}, u32[]{:S(2)}) collective-permute-start(bf16[4,4096]{1,0:T(4,128)(2,1)S(1)} %get-tuple-element.32), channel_id=1, source_target_pairs={{0,12},{4,8},{8,4},{12,0},{1,13},{5,9},{9,5},{13,1},{2,14},{6,10},... | collective-permute-start | bytes 98312 | tf_op jit(solution)/shard_map/ppermute | solution.py:36

commit v2 on v1

v2 whole, which is shorter than its diff:
```python
import functools
import math

import jax
import jax.numpy as jnp
import numpy as np
from jax import lax
from jax.experimental import pallas as pl
from jax.experimental.pallas import tpu as pltpu
from jax.sharding import PartitionSpec as P

HQ = 64
KVH = 4
DH = 128
GROUP = HQ // KVH
EPS = 1e-05
LOWEST = -1e30
FLOOR = -1e29
EXP2_SCALE = math.log2(math.e) / math.sqrt(DH)
ROWS_AXES = ("width", "sub")
F32 = jnp.float32
BF16 = jnp.bfloat16
VMEM = pl.BlockSpec(memory_space=pltpu.VMEM)
SMEM = pl.BlockSpec(memory_space=pltpu.SMEM)


def three_parts(value):
    high = value.astype(BF16).astype(F32)
    rest = value - high
    middle = rest.astype(BF16).astype(F32)
    return high, middle, rest - middle


def exchange(pieces, axes, count):
    arrived = [pieces[0]] * count
    for j in range(count - 1, 0, -1):
        arrived[j] = lax.ppermute(pieces[j], axes, [(i, i ^ j) for i in range(count)])
    return arrived


def prelude_kernel(first_ref):
    first_ref[...] = jnp.zeros_like(first_ref)


def rope_kernel(lengths_ref, frequency_ref, cosine_ref, sine_ref):
    rows = cosine_ref.shape[0]
    row = lax.broadcasted_iota(jnp.int32, (rows, DH), 0)
    lane = lax.broadcasted_iota(jnp.int32, (rows, DH), 1)
    position = jnp.zeros((rows, DH), jnp.int32)
    for r in range(rows):
        position = jnp.where(row == r, lengths_ref[r], position)
    angle = position.astype(F32) * frequency_ref[...]
    sine = jnp.sin(angle)
    cosine_ref[...] = jnp.cos(angle)
    sine_ref[...] = jnp.where(lane < DH // 2, -sine, sine)


def project_kernel(order, n_w, *refs):
    n_f = len(order)
    slots, (gain_ref, w_ref, _), outs = refs[:n_f], refs[n_f : n_f + 3], refs[n_f + 3 : n_f + 3 + n_w]
    lhs, result = refs[n_f + 3 + n_w :]
    rows = slots[0].shape[0]
    total = n_f * rows
    columns = w_ref.shape[1]
    widened = jnp.concatenate([slot[...].astype(F32) for slot in slots], axis=0)
    squares = jnp.sum(widened * widened, axis=1, keepdims=True)
    scaled = widened * gain_ref[...].astype(F32).reshape(1, -1)
    lhs[...] = scaled.astype(BF16)
    lane = lax.broadcasted_iota(jnp.int32, (total, 128), 1)
    stats = jnp.zeros((total, 128), F32)
    for at, part in enumerate(three_parts(squares)):
        stats = jnp.where(lane == at, part, stats)
    for k in range(n_f):
        result[order[k], :, :128] = stats[k * rows : (k + 1) * rows]
    product = jnp.dot(lhs[...], w_ref[...], preferred_element_type=F32)
    for k in range(n_f):
        result[order[k], :, 128:] = product[k * rows : (k + 1) * rows]
    mine = jnp.bitwise_xor(lax.axis_index("ffn"), lax.axis_index(ROWS_AXES))
    for j in range(n_w):
        outs[-1 - j][...] = result[jnp.bitwise_xor(mine, j)].astype(BF16)


def normalise_kernel(features, *refs):
    parts, out = refs[:-1], refs[-1]
    total = parts[0][...].astype(F32)
    for part in parts[1:]:
        total = total + part[...].astype(F32)
    squares = jnp.sum(total[:, :128], axis=1, keepdims=True)
    inverse_rms = 1.0 / jnp.sqrt(squares / features + EPS)
    out[...] = (total[:, 128:] * inverse_rms).astype(BF16)


def prepare(n_f, f, slots, cosine_ref, sine_ref, shards, heads, queries_ref, own_ref):
    rows, columns = slots[0].shape
    per = HQ // n_f
    for k in range(n_f):
        shards[jnp.bitwise_xor(f, k)] = slots[k][...].astype(F32)
    for h in range(HQ + 2 * KVH):
        at, end, found = h * DH, (h + 1) * DH, []
        while at < end:
            b, offset = divmod(at, columns)
            length = min(end - at, columns - offset)
            found.append(shards[b, :, offset : offset + length])
            at += length
        heads[:, h, :] = found[0] if len(found) == 1 else jnp.concatenate(found, axis=1)
    for r in range(rows):
        values = heads[r]
        turned = values * cosine_ref[r : r + 1, :] + pltpu.roll(values, DH // 2, 1) * sine_ref[r : r + 1, :]
        for b in range(n_f):
            queries_ref[b, r] = turned[b * per : (b + 1) * per].astype(BF16)
        new_keys = turned[HQ : HQ + KVH].astype(BF16).astype(F32)
        for g in range(KVH):
            own_ref[0, g, r : r + 1] = new_keys[g : g + 1]
            own_ref[1, g, r : r + 1] = values[HQ + KVH + g : HQ + KVH + g + 1]


def turn_keys_kernel(cache_ref, _, keys_ref):
    for r in range(keys_ref.shape[0]):
        keys_ref[r] = cache_ref[0, r].T


def attend(f, peers, queries_ref, own_ref, lengths_ref, keys_ref, cache_ref, outs, scores, probs):
    rows, per = queries_ref.shape[1:3]
    block = cache_ref.shape[2]
    position = f * block + lax.broadcasted_iota(jnp.int32, (1, block), 1)
    lane = lax.broadcasted_iota(jnp.int32, (per, 128), 1)
    theirs = [jnp.bitwise_xor(f, j) for j in peers]
    groups = [lax.div(b * per, GROUP) for b in theirs]
    for r in range(rows):
        for n, (b, g) in enumerate(zip(theirs, groups)):
            keys = keys_ref[r, pl.ds(pl.multiple_of(g * DH, DH), DH), :]
            scores[n, r] = jnp.dot(queries_ref[b, r], keys, preferred_element_type=F32)
    added, stats = {}, [jnp.zeros((per, 128), F32) for _ in peers]
    for r in range(rows):
        for n, (b, g) in enumerate(zip(theirs, groups)):
            raw = jnp.where(position < lengths_ref[r], scores[n, r], LOWEST)
            own = jnp.sum(queries_ref[b, r].astype(F32) * own_ref[0, g, r : r + 1], axis=1, keepdims=True)
            own = jnp.where(f == 0, own, LOWEST)
            top = jnp.maximum(jnp.maximum(jnp.max(raw, axis=1, keepdims=True), own), FLOOR)
            chances = jnp.exp2((raw - top) * EXP2_SCALE)
            own_chance = jnp.exp2((own - top) * EXP2_SCALE)
            totals = jnp.sum(chances, axis=1, keepdims=True) + own_chance
            probs[n, r] = chances.astype(BF16)
            added[n, r] = own_chance.astype(BF16).astype(F32) * own_ref[1, g, r : r + 1]
            for at, part in enumerate(three_parts(top) + three_parts(totals)):
                stats[n] = jnp.where(lane == 8 * r + at, part, stats[n])
    for r in range(rows):
        for n, g in enumerate(groups):
            values = cache_ref[1, r, :, pl.ds(pl.multiple_of(g * DH, DH), DH)]
            weighted = jnp.dot(probs[n, r], values, preferred_element_type=F32) + added[n, r]
            outs[n][r] = weighted.astype(BF16)
    for n in range(len(peers)):
        outs[n][rows] = stats[n].astype(BF16)


def attend_first_kernel(n_f, peers, *refs):
    slots = refs[:n_f]
    cosine_ref, sine_ref, lengths_ref, keys_ref, cache_ref, queries_ref, own_ref = refs[n_f : n_f + 7]
    outs, (shards, heads, scores, probs) = refs[n_f + 7 : -4], refs[-4:]
    f = lax.axis_index("ffn")
    prepare(n_f, f, slots, cosine_ref, sine_ref, shards, heads, queries_ref, own_ref)
    attend(f, peers, queries_ref, own_ref, lengths_ref, keys_ref, cache_ref, outs, scores, probs)


def attend_more_kernel(peers, queries_ref, own_ref, lengths_ref, keys_ref, cache_ref, *refs):
    attend(
        lax.axis_index("ffn"),
        peers,
        queries_ref,
        own_ref,
        lengths_ref,
        keys_ref,
        cache_ref,
        refs[:-2],
        *refs[-2:],
    )


def combine_kernel(*refs):
    parts, out = refs[:-1], refs[-1]
    rows = out.shape[0]

    def lane_sum(values, first):
        return sum(
            pltpu.roll(values, (128 - at) % 128, 1) if at else values for at in range(first, first + 3)
        )

    stats = [part[rows].astype(F32) for part in parts]
    tops = [lane_sum(values, 0) for values in stats]
    top = functools.reduce(jnp.maximum, tops)
    shares = [jnp.exp2((one - top) * EXP2_SCALE) for one in tops]
    total = sum(share * lane_sum(values, 3) for share, values in zip(shares, stats))
    for r in range(rows):
        at = slice(8 * r, 8 * r + 1)
        weighted = sum(share[:, at] * part[r].astype(F32) for share, part in zip(shares, parts))
        out[r] = (weighted / total[:, at]).astype(BF16)


def output_kernel(n_f, n_w, *refs):
    slots, w_ref, outs = refs[:n_w], refs[n_w], refs[n_w + 1 : n_w + 1 + n_f]
    wide, lhs, result = refs[n_w + 1 + n_f :]
    rows, per, _ = slots[0].shape
    columns = w_ref.shape[1]
    for j in range(n_w):
        wide[j * rows : (j + 1) * rows] = slots[j][...].astype(F32)
    for h in range(per):
        lhs[:, h * DH : (h + 1) * DH] = wide[:, h, :].astype(BF16)
    product = jnp.dot(lhs[...], w_ref[...], preferred_element_type=F32)
    for j in range(n_w):
        result[j] = product[j * rows : (j + 1) * rows]
    mine = jnp.bitwise_xor(lax.axis_index("ffn"), lax.axis_index(ROWS_AXES))
    for j in range(n_f):
        outs[-1 - j][...] = result[jnp.bitwise_xor(mine, j)].astype(BF16)


def sum_kernel(*refs):
    total = refs[0][...].astype(F32)
    for part in refs[1:-1]:
        total = total + part[...].astype(F32)
    refs[-1][...] = total.astype(BF16)


def call(kernel, outs, inputs, name, micros, scratch=(), smem=(), limit=4):
    many = isinstance(outs, list)
    return pl.pallas_call(
        kernel,
        out_shape=outs,
        in_specs=[SMEM if at in smem else VMEM for at in range(len(inputs))],
        out_specs=[VMEM] * len(outs) if many else VMEM,
        scratch_shapes=list(scratch),
        compiler_params=pltpu.CompilerParams(vmem_limit_bytes=limit << 20),
        cost_estimate=pl.CostEstimate(flops=int(micros * 1e9), bytes_accessed=0, transcendentals=0),
        name=name,
    )(*inputs)


def local(n_f, n_w, tokens, norm_gain, w_qkv, w_out, kv_cache, lengths):
    rows, features = tokens.shape
    columns, out_columns = w_qkv.shape[1], w_out.shape[1]
    per = HQ // n_f
    shape = jax.ShapeDtypeStruct
    w_qkv = pltpu.with_memory_space_constraint(w_qkv, pltpu.VMEM)
    w_out = pltpu.with_memory_space_constraint(w_out, pltpu.VMEM)
    kv_cache = pltpu.with_memory_space_constraint(kv_cache, pltpu.VMEM)
    half = 500000.0 ** (-(np.arange(DH // 2, dtype=np.float64) * 2.0 / DH))
    frequency = jnp.asarray(np.concatenate([half, half])[None, :], F32)

    token_slots = exchange([tokens] * n_f, "ffn", n_f)
    order = [0] + list(range(n_f - 1, 0, -1))
    first = call(prelude_kernel, shape((8, 128), F32), [], "prelude", 40)
    cosine, sine = call(
        rope_kernel, [shape((rows, DH), F32)] * 2, [lengths, frequency], "rope", 5, smem=(0,)
    )
    projected = call(
        functools.partial(project_kernel, order, n_w),
        [shape((rows, 128 + columns), BF16)] * n_w,
        [token_slots[k] for k in order] + [norm_gain, w_qkv, first],
        "project",
        20,
        scratch=[
            pltpu.VMEM((n_f * rows, features), BF16),
            pltpu.VMEM((n_f, rows, 128 + columns), F32),
        ],
    )
    partials = exchange(projected[::-1], ROWS_AXES, n_w)[::-1]
    qkv = call(
        functools.partial(normalise_kernel, float(features * n_w)),
        shape((rows, columns), BF16),
        partials,
        "normalise",
        10,
    )
    qkv_slots = exchange([qkv] * n_f, "ffn", n_f)
    keys = call(
        turn_keys_kernel,
        shape((rows, kv_cache.shape[3], kv_cache.shape[2]), BF16),
        [kv_cache, qkv],
        "turn_keys",
        5,
    )
    waves = [list(range(n_f - 1, 0, -1)), [0]]
    piece = shape((rows + 1, per, DH), BF16)
    room = [
        [pltpu.VMEM((len(peers), rows, per, kv_cache.shape[2]), kind) for kind in (F32, BF16)]
        for peers in waves
    ]
    queries, own, *found = call(
        functools.partial(attend_first_kernel, n_f, waves[0]),
        [shape((n_f, rows, per, DH), BF16), shape((2, KVH, rows, DH), F32)] + [piece] * len(waves[0]),
        qkv_slots + [cosine, sine, lengths, keys, kv_cache],
        "attend_first",
        20,
        scratch=[
            pltpu.VMEM((n_f, rows, columns), F32),
            pltpu.VMEM((rows, HQ + 2 * KVH, DH), F32),
        ]
        + room[0],
        smem=(n_f + 2,),
        limit=8,
    )
    attended = dict(zip(waves[0], found))
    for peers, rooms in zip(waves[1:], room[1:]):
        found = call(
            functools.partial(attend_more_kernel, peers),
            [piece] * len(peers),
            [queries, own, lengths, keys, kv_cache],
            "attend_more",
            5,
            scratch=rooms,
            smem=(2,),
        )
        attended.update(zip(peers, found))
    attended = [attended[j] for j in range(n_f)]
    attention = call(
        combine_kernel,
        shape((rows, per, DH), BF16),
        exchange(attended, "ffn", n_f)[::-1],
        "combine",
        10,
    )
    row_slots = exchange([attention] * n_w, ROWS_AXES, n_w)
    summands = call(
        functools.partial(output_kernel, n_f, n_w),
        [shape((rows, out_columns), BF16)] * n_f,
        row_slots + [w_out],
        "output",
        10,
        scratch=[
            pltpu.VMEM((n_w * rows, per, DH), F32),
            pltpu.VMEM((n_w * rows, per * DH), BF16),
            pltpu.VMEM((n_w, rows, out_columns), F32),
        ],
    )
    return call(
        sum_kernel, shape((rows, out_columns), BF16), exchange(summands[::-1], "ffn", n_f)[::-1], "total", 1
    )


def solution(mesh):
    placed = (
        P(("groups", "ffn"), ("width", "sub")),
        P(("width", "sub")),
        P(("width", "sub"), "ffn"),
        P("ffn", ("width", "sub")),
        P(None, ("groups", "width", "sub"), "ffn", None),
        P(("groups", "width", "sub")),
    )
    n_f, n_w = mesh.shape["ffn"], mesh.shape["width"] * mesh.shape["sub"]
    assert n_f == n_w and n_f & (n_f - 1) == 0
    return jax.shard_map(
        functools.partial(local, n_f, n_w),
        mesh=mesh,
        in_specs=placed,
        out_specs=P(("groups", "ffn"), ("width", "sub")),
        check_vma=False,
    )
```

time: 66.8 us -> 46.9 us (0.70)
  local copies, waits for them, and re-layouts: 11.2 us -> 0.04 us
  waiting for transfers between devices: 18.7 us -> 13.1 us
  Pallas kernels: 13.6 us -> 10.6 us
    unnamed x12 -> x22, local copies, waits for them, and re-layouts: 10.5 us -> 0.04 us
    ppermute x18, waiting for transfers between devices: 18.7 us -> 13.1 us  [exchange(): lax.ppermute(pieces[j], axes, [(i, i ^ j) for i in range(count)])]
    pallas_call x7 -> x10, Pallas kernels: 13.6 us -> 10.6 us  [call(): pl.pallas_call(kernel, out_shape=outs, in_specs=[SMEM if at in smem else...]
    reshape x1 -> x0, local copies, waits for them, and re-layouts: 0.71 us -> none  [local(): norm_gain.reshape(1, features)]
  transfers between devices with their start and end apart: 18 -> 18, of which waited for: 13 -> 13; matrix products, arithmetic and copies ran while one was open for 1% -> 0% of each run, Pallas kernels for 1% -> 6%
where the time goes in v2:
time: 46.9 us; the launch traced here: 46.7 us
  starting transfers between devices  22.9 us (49%)
  waiting for transfers between devices  13.1 us (28%)
  Pallas kernels  10.6 us (23%)
    ppermute x18, starting transfers between devices, exchange(): lax.ppermute(pieces[j], axes, [(i, i ^ j) for i in range(count)])  22.9 us
    ppermute x18, waiting for transfers between devices, exchange(): lax.ppermute(pieces[j], axes, [(i, i ^ j) for i in range(count)])  13.1 us
    pallas_call x10, Pallas kernels, call(): pl.pallas_call(kernel, out_shape=outs, in_specs=[SMEM if at in smem else...  10.6 us
  transfers between devices with their start and end apart: 18, of which 13 were waited for; matrix products, arithmetic and copies ran while one was open for 0% of the time, Pallas kernels for 6%

profile of v2, /device:TPU:0, one launch (start us, length us, event | category | flops | bytes accessed | tf_op | source)
XLA Modules:
  0.0 46.7 jit_solution(16912813534838497215)
XLA Ops:
  0.0 0.0 copy-start.1
  0.0 0.0 copy-start
  0.0 0.0 copy-start.2
  0.0 4.1 %collective-permute-start.1 = (bf16[4,4096]{1,0:T(4,128)(2,1)}, bf16[4,4096]{1,0:T(4,128)(2,1)S(1)}, u32[]{:S(2)}, u32[]{:S(2)}) collective-permute-start(bf16[4,4096]{1,0:T(4,128)(2,1)} %refs_0_.1), channel_id=1, source_target_pairs={{0,8},{4,12},{8,0},{12,4},{1,9},{5,13},{9,1},{13,5},{2,10},{6,14},... | collective-permute-start | bytes 98312 | tf_op jit(solution)/shard_map/ppermute | solution.py:37
  4.1 1.3 %collective-permute-start = (bf16[4,4096]{1,0:T(4,128)(2,1)}, bf16[4,4096]{1,0:T(4,128)(2,1)S(1)}, u32[]{:S(2)}, u32[]{:S(2)}) collective-permute-start(bf16[4,4096]{1,0:T(4,128)(2,1)} %refs_0_.1), channel_id=1, source_target_pairs={{0,12},{4,8},{8,4},{12,0},{1,13},{5,9},{9,5},{13,1},{2,14},{6,10},... | collective-permute-start | bytes 98312 | tf_op jit(solution)/shard_map/ppermute | solution.py:37
  5.5 0.2 collective-permute-start.2
  5.7 0.0 copy-start.3
  5.7 0.0 copy-start.4
  5.7 0.9 %collective-permute-done.1.refs_2_ = bf16[4,4096]{1,0:T(4,128)(2,1)S(1)} collective-permute-done((bf16[4,4096]{1,0:T(4,128)(2,1)}, bf16[4,4096]{1,0:T(4,128)(2,1)S(1)}, u32[]{:S(2)}, u32[]{:S(2)}) %collective-permute-start.1) | collective-permute-done | bytes 32800 | tf_op jit(solution)/shard_map/ppermute | solution.py:37
  6.6 3.5 %collective-permute-done.refs_1_ = bf16[4,4096]{1,0:T(4,128)(2,1)S(1)} collective-permute-done((bf16[4,4096]{1,0:T(4,128)(2,1)}, bf16[4,4096]{1,0:T(4,128)(2,1)S(1)}, u32[]{:S(2)}, u32[]{:S(2)}) %collective-permute-start) | collective-permute-done | bytes 32800 | tf_op jit(solution)/shard_map/ppermute | solution.py:37
  10.0 0.0 collective-permute-done.2.refs_3_
  10.0 0.0 copy-done.1
  10.0 0.0 copy-done
  10.0 0.0 copy-done.2
  10.1 2.6 %project.1 = (bf16[4,2432]{1,0:T(4,128)(2,1)S(1)}, bf16[4,2432]{1,0:T(4,128)(2,1)S(1)}, bf16[4,2432]{1,0:T(4,128)(2,1)S(1)}, bf16[4,2432]{1,0:T(4,128)(2,1)S(1)}) custom-call(bf16[4,4096]{1,0:T(4,128)(2,1)S(1)} %copy-done.1, bf16[4,4096]{1,0:T(4,128)(2,1)S(1)} %collective-permute-done.refs_1_, bf16[4,4096]{1,0:T(4,128)(2,1)S(1)} %collective-permute-done.1.refs_2_, ...), custom_call_target="tpu_custom_call" | custom-call | flops 20000000000 | tf_op jit(solution)/shard_map/project/pallas_call | solution.py:225
  12.6 0.1 collective-permute-start.3
  12.7 1.6 %collective-permute-start.4 = (bf16[4,2432]{1,0:T(4,128)(2,1)S(1)}, bf16[4,2432]{1,0:T(4,128)(2,1)S(1)}, u32[]{:S(2)}, u32[]{:S(2)}) collective-permute-start(bf16[4,2432]{1,0:T(4,128)(2,1)S(1)} %get-tuple-element.21), channel_id=1, source_target_pairs={{0,2},{1,3},{2,0},{3,1},{4,6},{5,7},{6,4},{7,5},{8,10},{9,11},{10,... | collective-permute-start | bytes 58376 | tf_op jit(solution)/shard_map/ppermute | solution.py:37
  14.3 0.3 collective-permute-start.5
  14.6 0.0 copy-done.3
  14.6 0.0 copy-done.4
  14.6 0.0 slice-start.4
  14.6 0.6 %rope.1 = (f32[4,128]{1,0:T(4,128)S(1)}, f32[4,128]{1,0:T(4,128)S(1)}) custom-call(s32[4]{0:T(128)S(1)} %copy-done.3, f32[1,128]{1,0:T(1,128)S(1)} %copy-done.4), custom_call_target="tpu_custom_call" | custom-call | flops 5000000000 | tf_op jit(solution)/shard_map/rope/pallas_call | solution.py:225
  15.2 0.9 %collective-permute-done.3.refs_0_ = bf16[4,2432]{1,0:T(4,128)(2,1)S(1)} collective-permute-done((bf16[4,2432]{1,0:T(4,128)(2,1)S(1)}, bf16[4,2432]{1,0:T(4,128)(2,1)S(1)}, u32[]{:S(2)}, u32[]{:S(2)}) %collective-permute-start.3) | collective-permute-done | bytes 19488 | tf_op jit(solution)/shard_map/ppermute | solution.py:37
  16.1 0.5 %collective-permute-done.4.refs_1_ = bf16[4,2432]{1,0:T(4,128)(2,1)S(1)} collective-permute-done((bf16[4,2432]{1,0:T(4,128)(2,1)S(1)}, bf16[4,2432]{1,0:T(4,128)(2,1)S(1)}, u32[]{:S(2)}, u32[]{:S(2)}) %collective-permute-start.4) | collective-permute-done | bytes 19488 | tf_op jit(solution)/shard_map/ppermute | solution.py:37
  16.6 0.0 collective-permute-done.5.refs_2_
  16.6 0.1 normalise.1._.refs_0_
  16.7 2.3 %collective-permute-start.8 = (bf16[4,2304]{1,0:T(4,128)(2,1)S(1)}, bf16[4,2304]{1,0:T(4,128)(2,1)S(1)}, u32[]{:S(2)}, u32[]{:S(2)}) collective-permute-start(bf16[4,2304]{1,0:T(4,128)(2,1)S(1)} %normalise.1._.refs_0_), channel_id=1, source_target_pairs={{0,12},{4,8},{8,4},{12,0},{1,13},{5,9},{9,5},{13,1},{2,14},{6,10},... | collective-permute-start | bytes 55304 | tf_op jit(solution)/shard_map/ppermute | solution.py:37
  19.0 0.0 collective-permute-start.7
  19.0 2.2 %collective-permute-start.6 = (bf16[4,2304]{1,0:T(4,128)(2,1)S(1)}, bf16[4,2304]{1,0:T(4,128)(2,1)S(1)}, u32[]{:S(2)}, u32[]{:S(2)}) collective-permute-start(bf16[4,2304]{1,0:T(4,128)(2,1)S(1)} %normalise.1._.refs_0_), channel_id=1, source_target_pairs={{0,4},{4,0},{8,12},{12,8},{1,5},{5,1},{9,13},{13,9},{2,6},{6,2},{1... | collective-permute-start | bytes 55304 | tf_op jit(solution)/shard_map/ppermute | solution.py:37
  21.1 0.0 slice-done.4
  21.1 0.0 slice-done.5
  21.2 1.2 %turn_keys.1.refs_7_.keys_ref = bf16[4,512,1024]{2,1,0:T(8,128)(2,1)S(1)} custom-call(bf16[2,4,1024,512]{3,2,1,0:T(8,128)(2,1)S(1)} %bitcast.3, bf16[4,2304]{1,0:T(4,128)(2,1)S(1)} %normalise.1._.refs_0_), custom_call_target="tpu_custom_call" | custom-call | flops 5000000000 | tf_op jit(solution)/shard_map/turn_keys/pallas_call | solution.py:225
  22.4 0.0 collective-permute-done.8.refs_3_
  22.4 1.2 %collective-permute-done.7.refs_2_ = bf16[4,2304]{1,0:T(4,128)(2,1)S(1)} collective-permute-done((bf16[4,2304]{1,0:T(4,128)(2,1)S(1)}, bf16[4,2304]{1,0:T(4,128)(2,1)S(1)}, u32[]{:S(2)}, u32[]{:S(2)}) %collective-permute-start.7) | collective-permute-done | bytes 18464 | tf_op jit(solution)/shard_map/ppermute | solution.py:37
  23.6 0.0 collective-permute-done.6.refs_1_
  23.6 1.8 %attend_first.1 = (bf16[4,4,16,128]{3,2,1,0:T(8,128)(2,1)S(1)}, f32[2,4,4,128]{3,2,1,0:T(4,128)S(1)}, bf16[5,16,128]{2,1,0:T(8,128)(2,1)S(1)}, bf16[5,16,128]{2,1,0:T(8,128)(2,1)S(1)}, bf16[5,16,128]{2,1,0:T(8,128)(2,1)S(1)}) custom-call(bf16[4,2304]{1,0:T(4,128)(2,1)S(1)} %normalise.1._.refs_0_, bf16[4,2304]{1,0:T(4,128)(2,1)S(1)} %collective-permute-done.6.refs_1_, ...), custom_call_target="tpu_custom_call" | custom-call | flops 20000000000 | tf_op jit(solution)/shard_map/attend_first/pallas_call | solution.py:225
  25.5 1.7 %collective-permute-start.9 = (bf16[5,16,128]{2,1,0:T(8,128)(2,1)S(1)}, bf16[5,16,128]{2,1,0:T(8,128)(2,1)S(1)}, u32[]{:S(2)}, u32[]{:S(2)}) collective-permute-start(bf16[5,16,128]{2,1,0:T(8,128)(2,1)S(1)} %get-tuple-element.26), channel_id=1, source_target_pairs={{0,12},{4,8},{8,4},{12,0},{1,13},{5,9},{9,5},{13,1},{2,14},{6,10},... | collective-permute-start | bytes 61448 | tf_op jit(solution)/shard_map/ppermute | solution.py:37
  27.2 1.1 %collective-permute-start.10 = (bf16[5,16,128]{2,1,0:T(8,128)(2,1)S(1)}, bf16[5,16,128]{2,1,0:T(8,128)(2,1)S(1)}, u32[]{:S(2)}, u32[]{:S(2)}) collective-permute-start(bf16[5,16,128]{2,1,0:T(8,128)(2,1)S(1)} %get-tuple-element.27), channel_id=1, source_target_pairs={{0,8},{4,12},{8,0},{12,4},{1,9},{5,13},{9,1},{13,5},{2,10},{6,14},... | collective-permute-start | bytes 61448 | tf_op jit(solution)/shard_map/ppermute | solution.py:37
  28.3 1.7 %collective-permute-start.11 = (bf16[5,16,128]{2,1,0:T(8,128)(2,1)S(1)}, bf16[5,16,128]{2,1,0:T(8,128)(2,1)S(1)}, u32[]{:S(2)}, u32[]{:S(2)}) collective-permute-start(bf16[5,16,128]{2,1,0:T(8,128)(2,1)S(1)} %get-tuple-element.28), channel_id=1, source_target_pairs={{0,4},{4,0},{8,12},{12,8},{1,5},{5,1},{9,13},{13,9},{2,6},{6,2},{1... | collective-permute-start | bytes 61448 | tf_op jit(solution)/shard_map/ppermute | solution.py:37
  29.9 1.0 %attend_more.1.refs_3_ = bf16[5,16,128]{2,1,0:T(8,128)(2,1)S(1)} custom-call(bf16[4,4,16,128]{3,2,1,0:T(8,128)(2,1)S(1)} %get-tuple-element.29.queries_ref, f32[2,4,4,128]{3,2,1,0:T(4,128)S(1)} %get-tuple-element.30.own_ref, s32[4]{0:T(128)S(1)} %copy-done.3, bf16[4,512,1024]{2,1,0:T(8,128)(2,1)S(1)} %turn_keys.1.refs_7_.keys_ref, ...), custom_call_target="tpu_custom_call" | custom-call | flops 5000000000 | tf_op jit(solution)/shard_map/attend_more/pallas_call | solution.py:225
  31.0 0.0 slice-start.2
  31.0 0.0 slice-start.3
  31.0 0.2 collective-permute-done.9.refs_0_
  31.2 0.7 %collective-permute-done.10.refs_1_ = bf16[5,16,128]{2,1,0:T(8,128)(2,1)S(1)} collective-permute-done((bf16[5,16,128]{2,1,0:T(8,128)(2,1)S(1)}, bf16[5,16,128]{2,1,0:T(8,128)(2,1)S(1)}, u32[]{:S(2)}, u32[]{:S(2)}) %collective-permute-start.10) | collective-permute-done | bytes 20512 | tf_op jit(solution)/shard_map/ppermute | solution.py:37
  31.8 0.2 collective-permute-done.11.refs_2_
  32.1 0.2 combine.1.refs_0_
  32.3 0.1 collective-permute-start.14
  32.4 1.5 %collective-permute-start.13 = (bf16[4,16,128]{2,1,0:T(8,128)(2,1)S(1)}, bf16[4,16,128]{2,1,0:T(8,128)(2,1)S(1)}, u32[]{:S(2)}, u32[]{:S(2)}) collective-permute-start(bf16[4,16,128]{2,1,0:T(8,128)(2,1)S(1)} %combine.1.refs_0_), channel_id=1, source_target_pairs={{0,2},{1,3},{2,0},{3,1},{4,6},{5,7},{6,4},{7,5},{8,10},{9,11},{10,... | collective-permute-start | bytes 49160 | tf_op jit(solution)/shard_map/ppermute | solution.py:37
  33.9 0.3 collective-permute-start.12
  34.2 1.5 %collective-permute-done.14.refs_3_ = bf16[4,16,128]{2,1,0:T(8,128)(2,1)S(1)} collective-permute-done((bf16[4,16,128]{2,1,0:T(8,128)(2,1)S(1)}, bf16[4,16,128]{2,1,0:T(8,128)(2,1)S(1)}, u32[]{:S(2)}, u32[]{:S(2)}) %collective-permute-start.14) | collective-permute-done | bytes 16416 | tf_op jit(solution)/shard_map/ppermute | solution.py:37
  35.7 0.5 %collective-permute-done.13.refs_2_ = bf16[4,16,128]{2,1,0:T(8,128)(2,1)S(1)} collective-permute-done((bf16[4,16,128]{2,1,0:T(8,128)(2,1)S(1)}, bf16[4,16,128]{2,1,0:T(8,128)(2,1)S(1)}, u32[]{:S(2)}, u32[]{:S(2)}) %collective-permute-start.13) | collective-permute-done | bytes 16416 | tf_op jit(solution)/shard_map/ppermute | solution.py:37
  36.2 0.0 collective-permute-done.12.refs_1_
  36.2 0.0 slice-done
  36.2 0.0 slice-done.1
  36.2 0.0 slice-done.2
  36.2 0.0 slice-done.3
  36.2 2.4 %output.1 = (bf16[4,4096]{1,0:T(4,128)(2,1)S(1)}, bf16[4,4096]{1,0:T(4,128)(2,1)S(1)}, bf16[4,4096]{1,0:T(4,128)(2,1)S(1)}, bf16[4,4096]{1,0:T(4,128)(2,1)S(1)}) custom-call(bf16[4,16,128]{2,1,0:T(8,128)(2,1)S(1)} %combine.1.refs_0_, bf16[4,16,128]{2,1,0:T(8,128)(2,1)S(1)} %collective-permute-done.12.refs_1_, ...), custom_call_target="tpu_custom_call" | custom-call | flops 10000000000 | tf_op jit(solution)/shard_map/output/pallas_call | solution.py:225
  38.6 2.3 %collective-permute-start.15 = (bf16[4,4096]{1,0:T(4,128)(2,1)S(1)}, bf16[4,4096]{1,0:T(4,128)(2,1)S(1)}, u32[]{:S(2)}, u32[]{:S(2)}) collective-permute-start(bf16[4,4096]{1,0:T(4,128)(2,1)S(1)} %get-tuple-element.31), channel_id=1, source_target_pairs={{0,12},{4,8},{8,4},{12,0},{1,13},{5,9},{9,5},{13,1},{2,14},{6,10},... | collective-permute-start | bytes 98312 | tf_op jit(solution)/shard_map/ppermute | solution.py:37
  40.9 0.9 %collective-permute-start.16 = (bf16[4,4096]{1,0:T(4,128)(2,1)S(1)}, bf16[4,4096]{1,0:T(4,128)(2,1)S(1)}, u32[]{:S(2)}, u32[]{:S(2)}) collective-permute-start(bf16[4,4096]{1,0:T(4,128)(2,1)S(1)} %get-tuple-element.32), channel_id=1, source_target_pairs={{0,8},{4,12},{8,0},{12,4},{1,9},{5,13},{9,1},{13,5},{2,10},{6,14},... | collective-permute-start | bytes 98312 | tf_op jit(solution)/shard_map/ppermute | solution.py:37
  41.7 1.3 %collective-permute-start.17 = (bf16[4,4096]{1,0:T(4,128)(2,1)S(1)}, bf16[4,4096]{1,0:T(4,128)(2,1)S(1)}, u32[]{:S(2)}, u32[]{:S(2)}) collective-permute-start(bf16[4,4096]{1,0:T(4,128)(2,1)S(1)} %get-tuple-element.33), channel_id=1, source_target_pairs={{0,4},{4,0},{8,12},{12,8},{1,5},{5,1},{9,13},{13,9},{2,6},{6,2},{1... | collective-permute-start | bytes 98312 | tf_op jit(solution)/shard_map/ppermute | solution.py:37
  43.0 1.7 %collective-permute-done.15.refs_0_ = bf16[4,4096]{1,0:T(4,128)(2,1)S(1)} collective-permute-done((bf16[4,4096]{1,0:T(4,128)(2,1)S(1)}, bf16[4,4096]{1,0:T(4,128)(2,1)S(1)}, u32[]{:S(2)}, u32[]{:S(2)}) %collective-permute-start.15) | collective-permute-done | bytes 32800 | tf_op jit(solution)/shard_map/ppermute | solution.py:37
  44.7 1.1 %collective-permute-done.16.refs_1_ = bf16[4,4096]{1,0:T(4,128)(2,1)S(1)} collective-permute-done((bf16[4,4096]{1,0:T(4,128)(2,1)S(1)}, bf16[4,4096]{1,0:T(4,128)(2,1)S(1)}, u32[]{:S(2)}, u32[]{:S(2)}) %collective-permute-start.16) | collective-permute-done | bytes 32800 | tf_op jit(solution)/shard_map/ppermute | solution.py:37
  45.8 0.3 collective-permute-done.17.refs_2_
  46.1 0.6 %total.1 = bf16[4,4096]{1,0:T(4,128)(2,1)} custom-call(bf16[4,4096]{1,0:T(4,128)(2,1)S(1)} %collective-permute-done.15.refs_0_, bf16[4,4096]{1,0:T(4,128)(2,1)S(1)} %collective-permute-done.16.refs_1_, bf16[4,4096]{1,0:T(4,128)(2,1)S(1)} %collective-permute-done.17.refs_2_, bf16[4,4096]{1,0:T(4,128)(2,1)S(1)} %get-tuple-element.34.refs_3_), custom_call_target="tpu_custom_call" | custom-call | flops 1000000000 | tf_op jit(solution)/shard_map/total/pallas_call | solution.py:225
  (6 shorter events, 0.0 us)
Async XLA Ops:
  0.0 10.0 %copy-start.1 = (bf16[4,4096]{1,0:T(4,128)(2,1)S(1)}, bf16[4,4096]{1,0:T(4,128)(2,1)}, u32[]{:S(2)}) copy-start(bf16[4,4096]{1,0:T(4,128)(2,1)} %refs_0_.1) | copy-start | bytes 98308
  0.0 10.0 %copy-start = (bf16[4096,2304]{1,0:T(8,128)(2,1)S(1)}, bf16[4096,2304]{1,0:T(8,128)(2,1)}, u32[]{:S(2)}) copy-start(bf16[4096,2304]{1,0:T(8,128)(2,1)} %refs_5_.1) | copy-start | bytes 56623108
  0.0 10.0 %copy-start.2 = (bf16[4096]{0:T(1024)(128)(2,1)S(1)}, bf16[4096]{0:T(1024)(128)(2,1)}, u32[]{:S(2)}) copy-start(bf16[4096]{0:T(1024)(128)(2,1)} %refs_4_.2) | copy-start | bytes 24580
  0.0 6.6 %collective-permute-start.1 = (bf16[4,4096]{1,0:T(4,128)(2,1)}, bf16[4,4096]{1,0:T(4,128)(2,1)S(1)}, u32[]{:S(2)}, u32[]{:S(2)}) collective-permute-start(bf16[4,4096]{1,0:T(4,128)(2,1)} %refs_0_.1), channel_id=1, source_target_pairs={{0,8},{4,12},{8,0},{12,4},{1,9},{5,13},{9,1},{13,5},{2,10},{6,14},... | collective-permute-start | bytes 98312 | tf_op jit(solution)/shard_map/ppermute | solution.py:37
  4.1 5.9 %collective-permute-start = (bf16[4,4096]{1,0:T(4,128)(2,1)}, bf16[4,4096]{1,0:T(4,128)(2,1)S(1)}, u32[]{:S(2)}, u32[]{:S(2)}) collective-permute-start(bf16[4,4096]{1,0:T(4,128)(2,1)} %refs_0_.1), channel_id=1, source_target_pairs={{0,12},{4,8},{8,4},{12,0},{1,13},{5,9},{9,5},{13,1},{2,14},{6,10},... | collective-permute-start | bytes 98312 | tf_op jit(solution)/shard_map/ppermute | solution.py:37
  5.5 4.6 %collective-permute-start.2 = (bf16[4,4096]{1,0:T(4,128)(2,1)}, bf16[4,4096]{1,0:T(4,128)(2,1)S(1)}, u32[]{:S(2)}, u32[]{:S(2)}) collective-permute-start(bf16[4,4096]{1,0:T(4,128)(2,1)} %refs_0_.1), channel_id=1, source_target_pairs={{0,4},{4,0},{8,12},{12,8},{1,5},{5,1},{9,13},{13,9},{2,6},{6,2},{1... | collective-permute-start | bytes 98312 | tf_op jit(solution)/shard_map/ppermute | solution.py:37
  5.7 8.9 %copy-start.3 = (s32[4]{0:T(128)S(1)}, s32[4]{0:T(128)}, u32[]{:S(2)}) copy-start(s32[4]{0:T(128)} %lengths_ref.3) | copy-start | bytes 52
  5.7 8.9 %copy-start.4 = (f32[1,128]{1,0:T(1,128)S(1)}, f32[1,128]{1,0:T(1,128)}, u32[]{:S(2)}) copy-start(f32[1,128]{1,0:T(1,128)} %constant.2.clone.frequency_ref) | copy-start | bytes 1540
  12.6 3.4 %collective-permute-start.3 = (bf16[4,2432]{1,0:T(4,128)(2,1)S(1)}, bf16[4,2432]{1,0:T(4,128)(2,1)S(1)}, u32[]{:S(2)}, u32[]{:S(2)}) collective-permute-start(bf16[4,2432]{1,0:T(4,128)(2,1)S(1)} %get-tuple-element.20), channel_id=1, source_target_pairs={{0,3},{1,2},{2,1},{3,0},{4,7},{5,6},{6,5},{7,4},{8,11},{9,10},{10,... | collective-permute-start | bytes 58376 | tf_op jit(solution)/shard_map/ppermute | solution.py:37
  12.7 3.8 %collective-permute-start.4 = (bf16[4,2432]{1,0:T(4,128)(2,1)S(1)}, bf16[4,2432]{1,0:T(4,128)(2,1)S(1)}, u32[]{:S(2)}, u32[]{:S(2)}) collective-permute-start(bf16[4,2432]{1,0:T(4,128)(2,1)S(1)} %get-tuple-element.21), channel_id=1, source_target_pairs={{0,2},{1,3},{2,0},{3,1},{4,6},{5,7},{6,4},{7,5},{8,10},{9,11},{10,... | collective-permute-start | bytes 58376 | tf_op jit(solution)/shard_map/ppermute | solution.py:37
  14.3 2.3 %collective-permute-start.5 = (bf16[4,2432]{1,0:T(4,128)(2,1)S(1)}, bf16[4,2432]{1,0:T(4,128)(2,1)S(1)}, u32[]{:S(2)}, u32[]{:S(2)}) collective-permute-start(bf16[4,2432]{1,0:T(4,128)(2,1)S(1)} %get-tuple-element.22), channel_id=1, source_target_pairs={{0,1},{1,0},{2,3},{3,2},{4,5},{5,4},{6,7},{7,6},{8,9},{9,8},{10,11... | collective-permute-start | bytes 58376 | tf_op jit(solution)/shard_map/ppermute | solution.py:37
  14.6 6.6 %slice-start.4 = ((s8[8388608]{0:T(1024)(128)(4,1)}), s8[4194304]{0:T(1024)(128)(4,1)S(1)}, s32[]{:S(2)}) async-start(s8[8388608]{0:T(1024)(128)(4,1)} %bitcast.2), calls=%async_computation.4 | async-start | bytes 8388608
  16.6 4.6 %slice-start.5 = ((s8[8388608]{0:T(1024)(128)(4,1)}), s8[4194304]{0:T(1024)(128)(4,1)S(1)}, s32[]{:S(2)}) async-start(s8[8388608]{0:T(1024)(128)(4,1)} %bitcast.2), calls=%async_computation.5 | async-start | bytes 8388608
  16.7 5.7 %collective-permute-start.8 = (bf16[4,2304]{1,0:T(4,128)(2,1)S(1)}, bf16[4,2304]{1,0:T(4,128)(2,1)S(1)}, u32[]{:S(2)}, u32[]{:S(2)}) collective-permute-start(bf16[4,2304]{1,0:T(4,128)(2,1)S(1)} %normalise.1._.refs_0_), channel_id=1, source_target_pairs={{0,12},{4,8},{8,4},{12,0},{1,13},{5,9},{9,5},{13,1},{2,14},{6,10},... | collective-permute-start | bytes 55304 | tf_op jit(solution)/shard_map/ppermute | solution.py:37
  19.0 4.7 %collective-permute-start.7 = (bf16[4,2304]{1,0:T(4,128)(2,1)S(1)}, bf16[4,2304]{1,0:T(4,128)(2,1)S(1)}, u32[]{:S(2)}, u32[]{:S(2)}) collective-permute-start(bf16[4,2304]{1,0:T(4,128)(2,1)S(1)} %normalise.1._.refs_0_), channel_id=1, source_target_pairs={{0,8},{4,12},{8,0},{12,4},{1,9},{5,13},{9,1},{13,5},{2,10},{6,14},... | collective-permute-start | bytes 55304 | tf_op jit(solution)/shard_map/ppermute | solution.py:37
  19.0 4.7 %collective-permute-start.6 = (bf16[4,2304]{1,0:T(4,128)(2,1)S(1)}, bf16[4,2304]{1,0:T(4,128)(2,1)S(1)}, u32[]{:S(2)}, u32[]{:S(2)}) collective-permute-start(bf16[4,2304]{1,0:T(4,128)(2,1)S(1)} %normalise.1._.refs_0_), channel_id=1, source_target_pairs={{0,4},{4,0},{8,12},{12,8},{1,5},{5,1},{9,13},{13,9},{2,6},{6,2},{1... | collective-permute-start | bytes 55304 | tf_op jit(solution)/shard_map/ppermute | solution.py:37
  25.5 5.7 %collective-permute-start.9 = (bf16[5,16,128]{2,1,0:T(8,128)(2,1)S(1)}, bf16[5,16,128]{2,1,0:T(8,128)(2,1)S(1)}, u32[]{:S(2)}, u32[]{:S(2)}) collective-permute-start(bf16[5,16,128]{2,1,0:T(8,128)(2,1)S(1)} %get-tuple-element.26), channel_id=1, source_target_pairs={{0,12},{4,8},{8,4},{12,0},{1,13},{5,9},{9,5},{13,1},{2,14},{6,10},... | collective-permute-start | bytes 61448 | tf_op jit(solution)/shard_map/ppermute | solution.py:37
  27.2 4.7 %collective-permute-start.10 = (bf16[5,16,128]{2,1,0:T(8,128)(2,1)S(1)}, bf16[5,16,128]{2,1,0:T(8,128)(2,1)S(1)}, u32[]{:S(2)}, u32[]{:S(2)}) collective-permute-start(bf16[5,16,128]{2,1,0:T(8,128)(2,1)S(1)} %get-tuple-element.27), channel_id=1, source_target_pairs={{0,8},{4,12},{8,0},{12,4},{1,9},{5,13},{9,1},{13,5},{2,10},{6,14},... | collective-permute-start | bytes 61448 | tf_op jit(solution)/shard_map/ppermute | solution.py:37
  28.3 3.8 %collective-permute-start.11 = (bf16[5,16,128]{2,1,0:T(8,128)(2,1)S(1)}, bf16[5,16,128]{2,1,0:T(8,128)(2,1)S(1)}, u32[]{:S(2)}, u32[]{:S(2)}) collective-permute-start(bf16[5,16,128]{2,1,0:T(8,128)(2,1)S(1)} %get-tuple-element.28), channel_id=1, source_target_pairs={{0,4},{4,0},{8,12},{12,8},{1,5},{5,1},{9,13},{13,9},{2,6},{6,2},{1... | collective-permute-start | bytes 61448 | tf_op jit(solution)/shard_map/ppermute | solution.py:37
  29.9 6.2 %slice-start = ((s8[16777216]{0:T(1024)(128)(4,1)}), s8[4194304]{0:T(1024)(128)(4,1)S(1)}, s32[]{:S(2)}) async-start(s8[16777216]{0:T(1024)(128)(4,1)} %bitcast), calls=%async_computation | async-start | bytes 8388608
  29.9 6.2 %slice-start.1 = ((s8[16777216]{0:T(1024)(128)(4,1)}), s8[4194304]{0:T(1024)(128)(4,1)S(1)}, s32[]{:S(2)}) async-start(s8[16777216]{0:T(1024)(128)(4,1)} %bitcast), calls=%async_computation.1 | async-start | bytes 8388608
  31.0 5.2 %slice-start.2 = ((s8[16777216]{0:T(1024)(128)(4,1)}), s8[4194304]{0:T(1024)(128)(4,1)S(1)}, s32[]{:S(2)}) async-start(s8[16777216]{0:T(1024)(128)(4,1)} %bitcast), calls=%async_computation.2 | async-start | bytes 8388608
  31.0 5.2 %slice-start.3 = ((s8[16777216]{0:T(1024)(128)(4,1)}), s8[4194304]{0:T(1024)(128)(4,1)S(1)}, s32[]{:S(2)}) async-start(s8[16777216]{0:T(1024)(128)(4,1)} %bitcast), calls=%async_computation.3 | async-start | bytes 8388608
  32.3 3.4 %collective-permute-start.14 = (bf16[4,16,128]{2,1,0:T(8,128)(2,1)S(1)}, bf16[4,16,128]{2,1,0:T(8,128)(2,1)S(1)}, u32[]{:S(2)}, u32[]{:S(2)}) collective-permute-start(bf16[4,16,128]{2,1,0:T(8,128)(2,1)S(1)} %combine.1.refs_0_), channel_id=1, source_target_pairs={{0,3},{1,2},{2,1},{3,0},{4,7},{5,6},{6,5},{7,4},{8,11},{9,10},{10,... | collective-permute-start | bytes 49160 | tf_op jit(solution)/shard_map/ppermute | solution.py:37
  32.4 3.8 %collective-permute-start.13 = (bf16[4,16,128]{2,1,0:T(8,128)(2,1)S(1)}, bf16[4,16,128]{2,1,0:T(8,128)(2,1)S(1)}, u32[]{:S(2)}, u32[]{:S(2)}) collective-permute-start(bf16[4,16,128]{2,1,0:T(8,128)(2,1)S(1)} %combine.1.refs_0_), channel_id=1, source_target_pairs={{0,2},{1,3},{2,0},{3,1},{4,6},{5,7},{6,4},{7,5},{8,10},{9,11},{10,... | collective-permute-start | bytes 49160 | tf_op jit(solution)/shard_map/ppermute | solution.py:37
  33.9 2.3 %collective-permute-start.12 = (bf16[4,16,128]{2,1,0:T(8,128)(2,1)S(1)}, bf16[4,16,128]{2,1,0:T(8,128)(2,1)S(1)}, u32[]{:S(2)}, u32[]{:S(2)}) collective-permute-start(bf16[4,16,128]{2,1,0:T(8,128)(2,1)S(1)} %combine.1.refs_0_), channel_id=1, source_target_pairs={{0,1},{1,0},{2,3},{3,2},{4,5},{5,4},{6,7},{7,6},{8,9},{9,8},{10,11... | collective-permute-start | bytes 49160 | tf_op jit(solution)/shard_map/ppermute | solution.py:37
  38.6 6.1 %collective-permute-start.15 = (bf16[4,4096]{1,0:T(4,128)(2,1)S(1)}, bf16[4,4096]{1,0:T(4,128)(2,1)S(1)}, u32[]{:S(2)}, u32[]{:S(2)}) collective-permute-start(bf16[4,4096]{1,0:T(4,128)(2,1)S(1)} %get-tuple-element.31), channel_id=1, source_target_pairs={{0,12},{4,8},{8,4},{12,0},{1,13},{5,9},{9,5},{13,1},{2,14},{6,10},... | collective-permute-start | bytes 98312 | tf_op jit(solution)/shard_map/ppermute | solution.py:37
  40.9 4.9 %collective-permute-start.16 = (bf16[4,4096]{1,0:T(4,128)(2,1)S(1)}, bf16[4,4096]{1,0:T(4,128)(2,1)S(1)}, u32[]{:S(2)}, u32[]{:S(2)}) collective-permute-start(bf16[4,4096]{1,0:T(4,128)(2,1)S(1)} %get-tuple-element.32), channel_id=1, source_target_pairs={{0,8},{4,12},{8,0},{12,4},{1,9},{5,13},{9,1},{13,5},{2,10},{6,14},... | collective-permute-start | bytes 98312 | tf_op jit(solution)/shard_map/ppermute | solution.py:37
  41.7 4.3 %collective-permute-start.17 = (bf16[4,4096]{1,0:T(4,128)(2,1)S(1)}, bf16[4,4096]{1,0:T(4,128)(2,1)S(1)}, u32[]{:S(2)}, u32[]{:S(2)}) collective-permute-start(bf16[4,4096]{1,0:T(4,128)(2,1)S(1)} %get-tuple-element.33), channel_id=1, source_target_pairs={{0,4},{4,0},{8,12},{12,8},{1,5},{5,1},{9,13},{13,9},{2,6},{6,2},{1... | collective-permute-start | bytes 98312 | tf_op jit(solution)/shard_map/ppermute | solution.py:37
